TPU v7x, 768 devices: a whole 4x8x12 slice. The times are simulated.
768 devices in a mesh: event: 16 (over y_hi, x), gx: 4 (over y_lo, core), gy: 12 (over z).
Axes of the slice: x: 4, y: 8 (y_hi: 4, y_lo: 2; y = y_hi * 2 + y_lo), z: 12, core: 2. Of those that a mesh axis runs over, the one named last changes fastest.
Arguments:
- forward_prev: float32 [16, 3, 64, 192, 128], P('event', None, 'gx', 'gy'), may hold values from -6 to 6
- forward_now: float32 [16, 3, 64, 192, 128], P('event', None, 'gx', 'gy'), may hold values from -6 to 6
- born_prev: float32 [16, 3, 64, 192, 128], P('event', None, 'gx', 'gy'), may hold values from -6 to 6
- born_now: float32 [16, 3, 64, 192, 128], P('event', None, 'gx', 'gy'), may hold values from -6 to 6
- adjoint_now: float32 [16, 3, 64, 192, 128], P('event', None, 'gx', 'gy'), may hold values from -6 to 6
- adjoint_next: float32 [16, 3, 64, 192, 128], P('event', None, 'gx', 'gy'), may hold values from -6 to 6
- shear_pert: float32 [64, 192, 128], P('gx', 'gy'), may hold values from -3 to 3
- lame_depth: float32 [128], replicated, may hold values from 0.5 to 2
- shear_depth: float32 [128], replicated, may hold values from 0.3 to 1.5
- buoyancy: float32 [128], replicated, may hold values from 0.5 to 2
- drm_cells: int32 [4, 12, 1024], P('gx', 'gy'), may hold values from 124 to 32767, as said below
- drm_matrix: float32 [3, 3, 4, 12, 1024], P(None, None, 'gx', 'gy'), may hold values from -12 to 12
- drm_motion: float32 [16, 3, 4, 12, 1024], P('event', None, 'gx', 'gy'), may hold values from -6 to 6
- source_cell: int32 [16], P('event'), may hold values from 0 to 1572863
- source_force: float32 [16, 3], P('event'), may hold values from -16 to 16
Outputs:
- hess_vec: float32 [64, 192, 128], P('gx', 'gy')
- forward_next: float32 [16, 3, 64, 192, 128], P('event', None, 'gx', 'gy')
- born_next: float32 [16, 3, 64, 192, 128], P('event', None, 'gx', 'gy')
- adjoint_prev: float32 [16, 3, 64, 192, 128], P('event', None, 'gx', 'gy')
Inputs may be any that keep to these rules, and one draw needn't show every extreme that they name: `drm_cells`: the 1024 entries of one tile are its distinct cells of the bottom 4 depth planes, each as (x * 16 + y) * 128 + z within the tile, in an order drawn from the seed.
All inputs are finite; a program needn't handle non-finite values.
Results may differ from a plain program's by a relative error of at most 0.0001.
Values sent between devices are 32-bit elements; how exact they have to be, the bound alone decides.
No kernel may reach another device: no remote copies, remote signals or barrier semaphores. Data moves between devices by JAX's collectives and lax.ppermute only.
A program may use at most 64 MiB of HBM per device.

v0:
```python
import jax
import jax.numpy as jnp
from jax import lax
from jax.sharding import PartitionSpec as P


def with_halo(cells, sides, width):
    for axis, dim in sides:
        count = lax.axis_size(axis)
        ends = count - 1
        head = lax.slice_in_dim(cells, 0, width, axis=dim)
        tail = lax.slice_in_dim(cells, cells.shape[dim] - width, cells.shape[dim], axis=dim)
        cells = jnp.concatenate(
            [
                lax.ppermute(tail, axis, [(i, (i + 1) % count) for i in range(ends)]),
                cells,
                lax.ppermute(head, axis, [((i + 1) % count, i) for i in range(ends)]),
            ],
            axis=dim,
        )
    return cells


def depth_derivative(interior):
    padded_z = jnp.pad(interior, [(0, 0)] * (interior.ndim - 1) + [(1, 1)])
    return (padded_z[..., 2:] - padded_z[..., :-2]) * 0.5


def gradient(padded):
    along_x = (padded[..., 2:, 1:-1, :] - padded[..., :-2, 1:-1, :]) * 0.5
    along_y = (padded[..., 1:-1, 2:, :] - padded[..., 1:-1, :-2, :]) * 0.5
    along_z = depth_derivative(padded[..., 1:-1, 1:-1, :])
    return jnp.stack([along_x, along_y, along_z], axis=-4)


def strain_pairs(gradients):

    def component(left_index, right_index):
        return gradients[..., left_index, right_index, :, :, :]

    return jnp.stack(
        [
            component(0, 0) + component(0, 0),
            component(1, 1) + component(1, 1),
            component(2, 2) + component(2, 2),
            component(0, 1) + component(1, 0),
            component(0, 2) + component(2, 0),
            component(1, 2) + component(2, 1),
        ],
        axis=-4,
    )


def stress(gradients, lame_depth, shear_depth):
    strain_sums = strain_pairs(gradients)
    trace_sum = (
        gradients[..., 0, 0, :, :, :]
        + gradients[..., 1, 1, :, :, :]
        + gradients[..., 2, 2, :, :, :]
    )
    normal_part = lame_depth * trace_sum
    return jnp.concatenate(
        [
            shear_depth * strain_sums[..., :3, :, :, :] + normal_part[..., None, :, :, :],
            shear_depth * strain_sums[..., 3:, :, :, :],
        ],
        axis=-4,
    )


def divergence(padded):

    def along_x(member):
        return (padded[..., member, 2:, 1:-1, :] - padded[..., member, :-2, 1:-1, :]) * 0.5

    def along_y(member):
        return (padded[..., member, 1:-1, 2:, :] - padded[..., member, 1:-1, :-2, :]) * 0.5

    def along_z(member):
        return depth_derivative(padded[..., member, 1:-1, 1:-1, :])

    force_x = along_x(0) + along_y(3) + along_z(4)
    force_y = along_x(3) + along_y(1) + along_z(5)
    force_z = along_x(4) + along_y(5) + along_z(2)
    return jnp.stack([force_x, force_y, force_z], axis=-4)


def advance(
    forces,
    events,
    forward_old,
    forward_mid,
    born_old,
    born_mid,
    adjoint_mid,
    adjoint_new,
    applied,
    buoyancy,
):
    depth_scale = 0.1 * buoyancy
    forward_new = 2.0 * forward_mid - forward_old + depth_scale * (forces[:events] + applied)
    born_new = 2.0 * born_mid - born_old + depth_scale * forces[events : 2 * events]
    surface = jnp.arange(forward_mid.shape[-1]) == 0
    received = jnp.where(surface, born_new, 0.0)
    adjoint_new_prev = (
        2.0 * adjoint_mid - adjoint_new + depth_scale * (forces[2 * events :] + received)
    )
    return (forward_new, born_new, adjoint_new_prev)


def exchange_final(forward_next, adjoint_prev):
    return with_halo(
        jnp.concatenate([forward_next, adjoint_prev], axis=0), (("gx", 2), ("gy", 3)), 1
    )


def on_device(
    forward_prev,
    forward_now,
    born_prev,
    born_now,
    adjoint_now,
    adjoint_next,
    shear_pert,
    lame_depth,
    shear_depth,
    buoyancy,
    drm_cells,
    drm_matrix,
    drm_motion,
    source_cell,
    source_force,
):
    events = forward_now.shape[0]
    cells_x = forward_now.shape[2]
    cells_y = forward_now.shape[3]
    cells_z = forward_now.shape[4]
    index_x = lax.axis_index("gx")
    index_y = lax.axis_index("gy")
    total_y = cells_y * lax.axis_size("gy")
    volume = cells_x * cells_y * cells_z
    element_cells = drm_cells.reshape(-1)
    matrix = drm_matrix.reshape(3, 3, -1)
    motion = drm_motion.reshape(events, 3, -1)
    element_force = jnp.sum(matrix[None] * motion[:, None], axis=2)
    drm_force = (
        jnp.zeros((events, 3, volume), jnp.float32).at[:, :, element_cells].add(element_force)
    )
    global_x = source_cell // (total_y * cells_z)
    global_y = source_cell // cells_z % total_y
    global_z = source_cell % cells_z
    local_x = global_x - index_x * cells_x
    local_y = global_y - index_y * cells_y
    present = (local_x >= 0) & (local_x < cells_x) & (local_y >= 0) & (local_y < cells_y)
    local_flat = (local_x * cells_y + local_y) * cells_z + global_z
    onehot = (
        (jnp.arange(volume, dtype=jnp.int32)[None, :] == local_flat[:, None]) & present[:, None]
    ).astype(jnp.float32)
    point_term = source_force[:, :, None] * onehot[:, None, :]
    applied = (drm_force + point_term).reshape(events, 3, cells_x, cells_y, cells_z)
    fields = jnp.concatenate([forward_now, born_now, adjoint_now], axis=0)
    padded = with_halo(fields, (("gx", 2), ("gy", 3)), 1)
    gradients = gradient(padded)
    stresses = stress(gradients, lame_depth, shear_depth)
    born_stress = stresses[events : 2 * events] + shear_pert * strain_pairs(gradients[:events])
    stresses = jnp.concatenate([stresses[:events], born_stress, stresses[2 * events :]], axis=0)
    stress_padded = with_halo(stresses, (("gx", 2), ("gy", 3)), 1)
    forces = divergence(stress_padded)
    forward_next, born_next, adjoint_prev = advance(
        forces,
        events,
        forward_prev,
        forward_now,
        born_prev,
        born_now,
        adjoint_now,
        adjoint_next,
        applied,
        buoyancy,
    )
    final_padded = exchange_final(forward_next, adjoint_prev)
    final_gradients = gradient(final_padded)
    paired = final_gradients[:events] + jnp.swapaxes(final_gradients[:events], 1, 2)
    product = jnp.sum(paired * final_gradients[events:], axis=(1, 2))
    local_sum = jnp.sum(-0.05 * product, axis=0)
    hess_vec = lax.psum(local_sum, "event")
    return (hess_vec, forward_next, born_next, adjoint_prev)


def solution(mesh):
    return jax.shard_map(
        on_device,
        mesh=mesh,
        in_specs=(
            P("event", None, "gx", "gy", None),
            P("event", None, "gx", "gy", None),
            P("event", None, "gx", "gy", None),
            P("event", None, "gx", "gy", None),
            P("event", None, "gx", "gy", None),
            P("event", None, "gx", "gy", None),
            P("gx", "gy", None),
            P(),
            P(),
            P(),
            P("gx", "gy", None),
            P(None, None, "gx", "gy", None),
            P("event", None, "gx", "gy", None),
            P("event"),
            P("event", None),
        ),
        out_specs=(
            P("gx", "gy", None),
            P("event", None, "gx", "gy", None),
            P("event", None, "gx", "gy", None),
            P("event", None, "gx", "gy", None),
        ),
        check_vma=False,
    )
```

profile of v0, /device:TPU:30, one launch (start us, length us, event | category | flops | bytes accessed | tf_op | source)
XLA Modules:
  0.0 301.7 jit_solution(8113133146397463726)
XLA Ops:
  7.2 1.1 constant_dynamic-update-slice_fusion.2
  8.3 1.0 constant_dynamic-update-slice_fusion.1
  9.4 1.9 collective-permute-start
  11.3 2.4 collective-permute-start.1
  14.5 15.0 %multiply_bitcast_fusion = f32[3,32768]{0,1:T(8,128)} fusion(f32[32768]{0:T(1024)S(1)} %fusion.68, f32[3]{0:T(128)S(1)} %bitcast.155), kind=kLoop, calls=%fused_computation.1 | loop fusion | flops 98304 | bytes 524300 | tf_op jit(solution)/shard_map/mul | solution.py:159
  29.6 1.3 collective-permute-start.2
  30.9 4.9 %collective-permute-start.3 = (f32[3,3,18,1,128]{4,3,2,1,0:T(1,128)S(1)}, f32[3,3,18,1,128]{4,3,2,1,0:T(1,128)S(1)}, u32[]{:S(2)}, u32[]{:S(2)}) collective-permute-start(f32[3,3,18,1,128]{4,3,2,1,0:T(1,128)S(1)} %get-tuple-element.19), channel_id=1, source_target_pairs={{0,1},{1,2},{2,3},{3,4},{4,5},{5,6},{6,7},{7,8},{8,9},{9,10},{10,1... | collective-permute-start | bytes 248840 | tf_op jit(solution)/shard_map/ppermute | solution.py:15
  35.9 0.5 collective-permute-done.2
  36.3 1.6 collective-permute-done.3
  37.9 1.0 fusion.9
  39.0 0.2 add_bitcast_fusion.2
  39.4 0.5 copy-done.13
  40.0 0.2 fusion.10
  40.3 0.7 copy-done.8
  40.9 0.2 fusion.17
  41.2 2.9 collective-permute-start.4
  44.1 1.9 collective-permute-start.5
  46.1 0.6 collective-permute-done.4
  46.8 3.8 %collective-permute-done.5 = f32[3,6,1,16,128]{4,3,2,0,1:T(8,128)S(1)} collective-permute-done((f32[3,6,1,16,128]{4,3,2,0,1:T(8,128)S(1)}, f32[3,6,1,16,128]{4,3,2,0,1:T(8,128)S(1)}, u32[]{:S(2)}, u32[]{:S(2)}) %collective-permute-start.5) | collective-permute-done | bytes 147488 | tf_op jit(solution)/shard_map/ppermute | solution.py:15
  50.6 0.9 pad_maximum_fusion.46
  51.5 1.3 collective-permute-start.6
  52.8 5.6 %collective-permute-start.7 = (f32[3,6,18,1,128]{4,3,2,0,1:T(1,128)}, f32[3,6,18,1,128]{4,3,2,0,1:T(1,128)}, u32[]{:S(2)}, u32[]{:S(2)}) collective-permute-start(f32[3,6,18,1,128]{4,3,2,0,1:T(1,128)} %get-tuple-element.7), channel_id=1, source_target_pairs={{0,1},{1,2},{2,3},{3,4},{4,5},{5,6},{6,7},{7,8},{8,9},{9,10},{10,1... | collective-permute-start | bytes 497672 | tf_op jit(solution)/shard_map/ppermute | solution.py:15
  58.4 1.0 copy.67
  59.4 17.3 %scatter_fusion = f32[3,32768]{0,1:T(8,128)} fusion(f32[3,32768]{0,1:T(8,128)} %multiply_bitcast_fusion, s32[1024]{0:T(1024)S(1)} %bitcast.154, f32[1024,3]{1,0:T(8,128)} %copy.67), kind=kCustom, calls=%fused_computation | custom fusion | flops 3072 | bytes 40960 | tf_op jit(solution)/shard_map/scatter-add | solution.py:147
  76.7 10.0 %copy.68 = f32[1,3,16,16,128]{4,3,2,1,0:T(8,128)S(1)} copy(f32[1,3,16,16,128]{1,4,3,2,0:T(8,128)} %bitcast.151) | data formatting | bytes 786432 | tf_op jit(solution)/shard_map/reshape | solution.py:160
  86.8 1.0 fusion.27
  87.9 1.0 fusion.31
  88.9 1.0 fusion.35
  90.1 0.9 copy-done.2
  90.9 0.1 copy-done.3
  91.1 0.1 copy-done.5
  91.2 0.1 copy-done.6
  91.3 0.1 copy-done.7
  91.4 1.1 fusion.38
  92.5 1.9 collective-permute-start.8
  94.4 2.4 collective-permute-start.9
  96.9 3.0 collective-permute-done.9
  99.9 1.3 collective-permute-start.10
  101.2 4.5 %collective-permute-start.11 = (f32[2,3,18,1,128]{4,3,2,1,0:T(1,128)S(1)}, f32[2,3,18,1,128]{4,3,2,1,0:T(1,128)S(1)}, u32[]{:S(2)}, u32[]{:S(2)}) collective-permute-start(f32[2,3,18,1,128]{4,3,2,1,0:T(1,128)S(1)} %get-tuple-element.32), channel_id=1, source_target_pairs={{0,1},{1,2},{2,3},{3,4},{4,5},{5,6},{6,7},{7,8},{8,9},{9,10},{10,1... | collective-permute-start | bytes 165896 | tf_op jit(solution)/shard_map/ppermute | solution.py:15
  105.8 0.2 collective-permute-done.10
  106.0 1.6 collective-permute-done.11
  107.6 0.3 fusion.23
  107.9 0.5 fusion.14
  108.4 0.2 pad_maximum_fusion
  108.7 0.2 fusion.3
  108.9 0.7 broadcast_multiply_fusion
  109.6 183.7 %all-reduce.7.cloned.1.call-done = f32[16,16,128]{2,1,0:T(8,128)} async-done(((f32[16,16,128]{2,1,0:T(8,128)}), f32[16,16,128]{2,1,0:T(8,128)}) %all-reduce.7.cloned.1.call-update) | async-done | bytes 131088 | tf_op jit(solution)/shard_map/psum | solution.py:186
  293.3 1.6 copy.97
  (55 shorter events, 1.0 us)
Async XLA Ops:
  7.2 2.2 copy-start.4
  7.2 286.1 %all-reduce.7.cloned.1.call-start = ((), (), s32[]{:S(2)}) async-start(), calls=%async_computation | async-start | bytes 262144 | tf_op jit(solution)/shard_map/psum | solution.py:186
  8.3 6.2 %copy-start.12 = (f32[1,3]{1,0:T(1,128)S(1)}, f32[1,3]{1,0:T(1,128)}, u32[]{:S(2)}) copy-start(f32[1,3]{1,0:T(1,128)} %param.29) | copy-start | bytes 40
  9.4 20.1 %collective-permute-start = (f32[3,3,1,16,128]{4,3,2,1,0:T(8,128)S(1)}, f32[3,3,1,16,128]{4,3,2,1,0:T(8,128)S(1)}, u32[]{:S(2)}, u32[]{:S(2)}) collective-permute-start(f32[3,3,1,16,128]{4,3,2,1,0:T(8,128)S(1)} %get-tuple-element.28), channel_id=1, source_target_pairs={{12,0},{24,12},{36,24},{13,1},{25,13},{37,25},{14,2},{26,14},{38,2... | collective-permute-start | bytes 221192 | tf_op jit(solution)/shard_map/ppermute | solution.py:17
  11.3 18.2 %collective-permute-start.1 = (f32[3,3,1,16,128]{4,3,2,1,0:T(8,128)S(1)}, f32[3,3,1,16,128]{4,3,2,1,0:T(8,128)S(1)}, u32[]{:S(2)}, u32[]{:S(2)}) collective-permute-start(f32[3,3,1,16,128]{4,3,2,1,0:T(8,128)S(1)} %get-tuple-element.27), channel_id=1, source_target_pairs={{0,12},{12,24},{24,36},{1,13},{13,25},{25,37},{2,14},{14,26},{26,3... | collective-permute-start | bytes 221192 | tf_op jit(solution)/shard_map/ppermute | solution.py:15
  29.5 6.4 %copy-start.11 = (s32[1,1,1024]{2,1,0:T(1,128)S(1)}, s32[1,1,1024]{2,1,0:T(1,128)}, u32[]{:S(2)}) copy-start(s32[1,1,1024]{2,1,0:T(1,128)} %param.25) | copy-start | bytes 12292
  29.6 6.7 %collective-permute-start.2 = (f32[3,3,18,1,128]{4,3,2,1,0:T(1,128)S(1)}, f32[3,3,18,1,128]{4,3,2,1,0:T(1,128)S(1)}, u32[]{:S(2)}, u32[]{:S(2)}) collective-permute-start(f32[3,3,18,1,128]{4,3,2,1,0:T(1,128)S(1)} %get-tuple-element.18), channel_id=1, source_target_pairs={{1,0},{2,1},{3,2},{4,3},{5,4},{6,5},{7,6},{8,7},{9,8},{10,9},{11,1... | collective-permute-start | bytes 248840 | tf_op jit(solution)/shard_map/ppermute | solution.py:17
  30.9 7.0 %collective-permute-start.3 = (f32[3,3,18,1,128]{4,3,2,1,0:T(1,128)S(1)}, f32[3,3,18,1,128]{4,3,2,1,0:T(1,128)S(1)}, u32[]{:S(2)}, u32[]{:S(2)}) collective-permute-start(f32[3,3,18,1,128]{4,3,2,1,0:T(1,128)S(1)} %get-tuple-element.19), channel_id=1, source_target_pairs={{0,1},{1,2},{2,3},{3,4},{4,5},{5,6},{6,7},{7,8},{8,9},{9,10},{10,1... | collective-permute-start | bytes 248840 | tf_op jit(solution)/shard_map/ppermute | solution.py:15
  39.2 0.7 copy-start.13
  39.4 0.7 copy-start.14
  40.0 0.9 copy-start.8
  41.2 4.9 %copy-start.15 = (f32[128]{0:T(128)S(1)}, f32[128]{0:T(128)}, u32[]{:S(2)}) copy-start(f32[128]{0:T(128)} %param.24) | copy-start | bytes 1540
  41.2 4.9 %copy-start.10 = (f32[1,3,1,1,1024]{4,3,2,1,0:T(1,128)S(1)}, f32[1,3,1,1,1024]{4,3,2,1,0:T(1,128)}, u32[]{:S(2)}) copy-start(f32[1,3,1,1,1024]{4,3,2,1,0:T(1,128)} %param.27) | copy-start | bytes 36868
  41.2 4.9 %copy-start.9 = (f32[3,3,1,1,1024]{4,3,2,1,0:T(1,128)S(1)}, f32[3,3,1,1,1024]{4,3,2,1,0:T(1,128)}, u32[]{:S(2)}) copy-start(f32[3,3,1,1,1024]{4,3,2,1,0:T(1,128)} %param.26) | copy-start | bytes 110596
  41.2 5.5 %collective-permute-start.4 = (f32[3,6,1,16,128]{4,3,2,0,1:T(8,128)S(1)}, f32[3,6,1,16,128]{4,3,2,0,1:T(8,128)S(1)}, u32[]{:S(2)}, u32[]{:S(2)}) collective-permute-start(f32[3,6,1,16,128]{4,3,2,0,1:T(8,128)S(1)} %get-tuple-element.12), channel_id=1, source_target_pairs={{12,0},{24,12},{36,24},{13,1},{25,13},{37,25},{14,2},{26,14},{38,2... | collective-permute-start | bytes 442376 | tf_op jit(solution)/shard_map/ppermute | solution.py:17
  44.1 6.5 %collective-permute-start.5 = (f32[3,6,1,16,128]{4,3,2,0,1:T(8,128)S(1)}, f32[3,6,1,16,128]{4,3,2,0,1:T(8,128)S(1)}, u32[]{:S(2)}, u32[]{:S(2)}) collective-permute-start(f32[3,6,1,16,128]{4,3,2,0,1:T(8,128)S(1)} %get-tuple-element.11), channel_id=1, source_target_pairs={{0,12},{12,24},{24,36},{1,13},{13,25},{25,37},{2,14},{14,26},{26,3... | collective-permute-start | bytes 442376 | tf_op jit(solution)/shard_map/ppermute | solution.py:15
  51.5 35.3 %collective-permute-start.6 = (f32[3,6,18,1,128]{4,3,2,0,1:T(1,128)}, f32[3,6,18,1,128]{4,3,2,0,1:T(1,128)}, u32[]{:S(2)}, u32[]{:S(2)}) collective-permute-start(f32[3,6,18,1,128]{4,3,2,0,1:T(1,128)} %get-tuple-element.6), channel_id=1, source_target_pairs={{1,0},{2,1},{3,2},{4,3},{5,4},{6,5},{7,6},{8,7},{9,8},{10,9},{11,1... | collective-permute-start | bytes 497672 | tf_op jit(solution)/shard_map/ppermute | solution.py:17
  52.8 34.0 %collective-permute-start.7 = (f32[3,6,18,1,128]{4,3,2,0,1:T(1,128)}, f32[3,6,18,1,128]{4,3,2,0,1:T(1,128)}, u32[]{:S(2)}, u32[]{:S(2)}) collective-permute-start(f32[3,6,18,1,128]{4,3,2,0,1:T(1,128)} %get-tuple-element.7), channel_id=1, source_target_pairs={{0,1},{1,2},{2,3},{3,4},{4,5},{5,6},{6,7},{7,8},{8,9},{9,10},{10,1... | collective-permute-start | bytes 497672 | tf_op jit(solution)/shard_map/ppermute | solution.py:15
  89.9 1.0 copy-start.2
  89.9 1.1 copy-start.3
  90.0 1.2 copy-start.5
  90.0 1.3 copy-start.6
  90.0 1.4 copy-start.7
  92.5 15.4 %copy-start = (f32[1,3,16,16,128]{4,3,2,1,0:T(8,128)}, f32[1,3,16,16,128]{4,3,2,1,0:T(8,128)S(1)}, u32[]{:S(2)}) copy-start(f32[1,3,16,16,128]{4,3,2,1,0:T(8,128)S(1)} %get-tuple-element.41) | copy-start | bytes 1179652
  92.5 15.4 %copy-start.1 = (f32[1,3,16,16,128]{4,3,2,1,0:T(8,128)}, f32[1,3,16,16,128]{4,3,2,1,0:T(8,128)S(1)}, u32[]{:S(2)}) copy-start(f32[1,3,16,16,128]{4,3,2,1,0:T(8,128)S(1)} %get-tuple-element.39) | copy-start | bytes 1179652
  92.5 4.3 %collective-permute-start.8 = (f32[2,3,1,16,128]{4,3,2,1,0:T(8,128)S(1)}, f32[2,3,1,16,128]{4,3,2,1,0:T(8,128)S(1)}, u32[]{:S(2)}, u32[]{:S(2)}) collective-permute-start(f32[2,3,1,16,128]{4,3,2,1,0:T(8,128)S(1)} %get-tuple-element.35), channel_id=1, source_target_pairs={{12,0},{24,12},{36,24},{13,1},{25,13},{37,25},{14,2},{26,14},{38,2... | collective-permute-start | bytes 147464 | tf_op jit(solution)/shard_map/ppermute | solution.py:17
  94.4 5.4 %collective-permute-start.9 = (f32[2,3,1,16,128]{4,3,2,1,0:T(8,128)S(1)}, f32[2,3,1,16,128]{4,3,2,1,0:T(8,128)S(1)}, u32[]{:S(2)}, u32[]{:S(2)}) collective-permute-start(f32[2,3,1,16,128]{4,3,2,1,0:T(8,128)S(1)} %get-tuple-element.34), channel_id=1, source_target_pairs={{0,12},{12,24},{24,36},{1,13},{13,25},{25,37},{2,14},{14,26},{26,3... | collective-permute-start | bytes 147464 | tf_op jit(solution)/shard_map/ppermute | solution.py:15
  99.9 6.0 %collective-permute-start.10 = (f32[2,3,18,1,128]{4,3,2,1,0:T(1,128)S(1)}, f32[2,3,18,1,128]{4,3,2,1,0:T(1,128)S(1)}, u32[]{:S(2)}, u32[]{:S(2)}) collective-permute-start(f32[2,3,18,1,128]{4,3,2,1,0:T(1,128)S(1)} %get-tuple-element.31), channel_id=1, source_target_pairs={{1,0},{2,1},{3,2},{4,3},{5,4},{6,5},{7,6},{8,7},{9,8},{10,9},{11,1... | collective-permute-start | bytes 165896 | tf_op jit(solution)/shard_map/ppermute | solution.py:17
  101.2 6.3 %collective-permute-start.11 = (f32[2,3,18,1,128]{4,3,2,1,0:T(1,128)S(1)}, f32[2,3,18,1,128]{4,3,2,1,0:T(1,128)S(1)}, u32[]{:S(2)}, u32[]{:S(2)}) collective-permute-start(f32[2,3,18,1,128]{4,3,2,1,0:T(1,128)S(1)} %get-tuple-element.32), channel_id=1, source_target_pairs={{0,1},{1,2},{2,3},{3,4},{4,5},{5,6},{6,7},{7,8},{8,9},{9,10},{10,1... | collective-permute-start | bytes 165896 | tf_op jit(solution)/shard_map/ppermute | solution.py:15
Sparse Core Ops, SparseCore 0:
  109.7 183.5 all-reduce.6
where the time goes:
time: 303 us; the launch traced here: 302 us
  waiting for transfers between devices  195 us (64%)
  other arithmetic  41.7 us (14%)
  starting transfers between devices  32.4 us (11%)
  local copies, waits for them, and re-layouts  17.4 us (6%)
  between operations  15.3 us (5%)
    psum x1, waiting for transfers between devices, on_device(): hess_vec = lax.psum(local_sum, 'event')  184 us
    ppermute x6, starting transfers between devices, with_halo(): lax.ppermute(tail, axis, [(i, (i + 1) % count) for i in range(ends)])  21.8 us
    scatter-add x1, other arithmetic, on_device(): jnp.zeros((events, 3, volume), jnp.float32).at[:, :, element_cells]  17.3 us
    mul x1, other arithmetic, on_device(): point_term = source_force[:, :, None] * onehot[:, None, :]  15 us
    ppermute x6, starting transfers between devices, with_halo(): lax.ppermute(head, axis, [((i + 1) % count, i) for i in range(ends)])  10.6 us
    reshape x1, local copies, waits for them, and re-layouts, on_device(): (drm_force + point_term).reshape(events, 3, cells_x, cells_y, cells_z)  9.98 us
    ppermute x6, waiting for transfers between devices, with_halo(): lax.ppermute(tail, axis, [(i, (i + 1) % count) for i in range(ends)])  9.95 us
    unnamed x36, local copies, waits for them, and re-layouts  6.27 us
  transfers between devices with their start and end apart: 13, of which 8 were waited for; matrix products, arithmetic and copies ran while one was open for 14% of the time, Pallas kernels for 0%

commit v1 on v0

v1 whole, which is shorter than its diff:
```python
import jax
import jax.numpy as jnp
from jax import lax
from jax.experimental import pallas as pl
from jax.experimental.pallas import tpu as pltpu
from jax.sharding import PartitionSpec as P

X = 16
Y = 16
Z = 128
CELLS = X * Y
LAYER = 4
ELEMS = CELLS * LAYER

Y_BASE = 27
Y_PERT = 33
Y_PLANES = 35

X_STEP = 54
X_PERT = 9 * X_STEP
X_BASE = X_PERT + 34
X_ROWS = X_BASE + 6 * Y

ROWS = 32
ZERO = 8

F32 = jnp.float32


def now_row(c, d):
    return c * X_STEP + (0, 20, 38)[d - 1]


def pert_row(d):
    return X_PERT + (0, 18)[d - 1]


def near_x(high, d):
    return jnp.where(high, X - d, d - 1)


def begin_kernel(
    place_ref,
    *refs,
):
    sources, refs = refs[:13], refs[13:]
    base_ref, low_ref, high_ref, xa_ref, xb_ref, applied_ref = refs[:6]
    held, arrived = refs[6:19], refs[19]
    copies = [
        pltpu.make_async_copy(source, ref, arrived.at[i])
        for i, (source, ref) in enumerate(zip(sources, held))
    ]
    for i in (8, 9, 10, 11, 12, 7, 6, 0, 1, 2, 3, 4, 5):
        copies[i].start()
    fprev_ref, fnow_ref, bprev_ref, bnow_ref, anow_ref, anext_ref = held[:6]
    pert_ref, buoy_ref, cells_ref, matrix_ref, motion_ref, cell_ref, force_ref = held[6:]
    for i in (8, 9, 10, 11, 12):
        copies[i].wait()

    index_x = place_ref[0]
    index_y = place_ref[1]
    total_y = place_ref[2]

    cells = cells_ref[...].reshape(1, ELEMS)
    column = cells // Z
    depth = cells % Z
    pick = jnp.where(
        lax.broadcasted_iota(jnp.int32, (CELLS, ELEMS), 0) == column, 1.0, 0.0
    ).astype(jnp.bfloat16)
    slot = lax.broadcasted_iota(jnp.int32, (16, ELEMS), 0)
    spread = jnp.zeros((16, ELEMS), F32)
    for i in range(3):
        element = sum(
            matrix_ref[3 * i + c].reshape(1, ELEMS) * motion_ref[c].reshape(1, ELEMS)
            for c in range(3)
        )
        spread = jnp.where(slot == depth - (Z - 16) - 4 * i, element, spread)
    spread = jnp.concatenate([jnp.zeros((Z - 16, ELEMS), F32), spread], axis=0)
    placed = jnp.zeros((CELLS, Z), F32)
    rest = spread
    for _ in range(3):
        part = rest.astype(jnp.bfloat16)
        placed = placed + lax.dot_general(
            pick, part, (((1,), (1,)), ((), ())), preferred_element_type=F32
        )
        rest = rest - part.astype(F32)
    lane = lax.broadcasted_iota(jnp.int32, (CELLS, Z), 1)
    for i in range(3):
        moved = placed if i == 0 else pltpu.roll(placed, 4 * i, 1)
        applied_ref[i] = jnp.where(lane >= Z - LAYER, moved, 0.0)

    cell = cell_ref[0]
    local_x = cell // (total_y * Z) - index_x * X
    local_y = (cell // Z) % total_y - index_y * Y
    inside = (local_x >= 0) & (local_x < X) & (local_y >= 0) & (local_y < Y)

    @pl.when(inside)
    def _():
        row = local_x * Y + local_y
        here = lax.broadcasted_iota(jnp.int32, (1, Z), 1) == cell % Z
        for i in range(3):
            old = applied_ref[i, pl.ds(row, 1), :]
            applied_ref[i, pl.ds(row, 1), :] = old + jnp.where(here, force_ref[:, i : i + 1], 0.0)

    for i in (7, 6, 0, 1, 2, 3, 4, 5):
        copies[i].wait()
    scale = 0.1 * buoy_ref[...].reshape(1, Z)
    surface_scale = jnp.where(lane[:1] == 0, scale, 0.0)
    for i in range(3):
        base_ref[i] = 2.0 * fnow_ref[i] - fprev_ref[i] + scale * applied_ref[i]
        born = 2.0 * bnow_ref[i] - bprev_ref[i]
        base_ref[3 + i] = born
        base_ref[6 + i] = 2.0 * anow_ref[i] - anext_ref[i] + surface_scale * born

    now = [r.at[i] for r in (fnow_ref, bnow_ref, anow_ref) for i in range(3)]
    bases = [base_ref.at[i] for i in (0, 1, 2, 6, 7, 8)]

    def column_of(ref, y):
        return ref[pl.ds(y, X, stride=Y), :]

    for c in range(9):
        for k in range(3):
            low_ref[3 * c + k] = column_of(now[c], k)
            high_ref[3 * c + k] = column_of(now[c], Y - 3 + k)
    for c in range(6):
        low_ref[Y_BASE + c] = column_of(bases[c], 0)
        high_ref[Y_BASE + c] = column_of(bases[c], Y - 1)
    for k in range(2):
        low_ref[Y_PERT + k] = column_of(pert_ref, k)
        high_ref[Y_PERT + k] = column_of(pert_ref, Y - 2 + k)

    odd = index_x % 2 == 1
    for ref, high in ((xa_ref, jnp.logical_not(odd)), (xb_ref, odd)):

        def plane_of(source, d):
            start = pl.multiple_of(near_x(high, d) * Y, Y)
            return source[pl.ds(start, Y), :]

        for c in range(9):
            for d in (1, 2, 3):
                ref[pl.ds(now_row(c, d) + 3 - d, Y), :] = plane_of(now[c], d)
        for d in (1, 2):
            ref[pl.ds(pert_row(d) + 2 - d, Y), :] = plane_of(pert_ref, d)
        for c in range(6):
            ref[pl.ds(X_BASE + c * Y, Y), :] = plane_of(bases[c], 1)


def widen_kernel(place_ref, xa_in, xb_in, left_ref, right_ref, xa_ref, xb_ref):
    odd = place_ref[0] % 2 == 1
    for source, ref, high in ((xa_in, xa_ref, jnp.logical_not(odd)), (xb_in, xb_ref, odd)):
        ref[...] = source[...]
        for d in (1, 2):
            x = near_x(high, d)
            for c in range(9):
                start = now_row(c, d)
                for k in range(3 - d):
                    ref[pl.ds(start + k, 1), :] = left_ref[3 * c + d + k, pl.ds(x, 1), :]
                    ref[pl.ds(start + 19 - d + k, 1), :] = right_ref[3 * c + k, pl.ds(x, 1), :]
        x = near_x(high, 1)
        ref[pl.ds(pert_row(1), 1), :] = left_ref[Y_PERT + 1, pl.ds(x, 1), :]
        ref[pl.ds(pert_row(1) + 17, 1), :] = right_ref[Y_PERT, pl.ds(x, 1), :]


def step_kernel(
    place_ref,
    fnow_ref,
    bnow_ref,
    anow_ref,
    pert_in,
    base_ref,
    left_ref,
    right_ref,
    xa_ref,
    xb_ref,
    lame_ref,
    shear_ref,
    buoy_ref,
    hess_ref,
    fnext_ref,
    bnext_ref,
    aprev_ref,
    wide,
    pert,
    stress,
    new,
):
    index_x = place_ref[0]
    index_y = place_ref[1]
    last_x = place_ref[3] - 1
    last_y = place_ref[4] - 1

    now = [r.at[i] for r in (fnow_ref, bnow_ref, anow_ref) for i in range(3)]
    for c in range(9):
        for x in range(X):
            wide[c, pl.ds((x + 3) * ROWS + ZERO, Y), :] = now[c][pl.ds(x * Y, Y), :]
        for k in range(3):
            wide[c, pl.ds(3 * ROWS + ZERO - 3 + k, X, stride=ROWS), :] = left_ref[3 * c + k]
            wide[c, pl.ds(3 * ROWS + ZERO + Y + k, X, stride=ROWS), :] = right_ref[3 * c + k]
    for x in range(X):
        pert[pl.ds((x + 2) * ROWS + ZERO, Y), :] = pert_in[pl.ds(x * Y, Y), :]
    for k in range(2):
        pert[pl.ds(2 * ROWS + ZERO - 2 + k, X, stride=ROWS), :] = left_ref[Y_PERT + k]
        pert[pl.ds(2 * ROWS + ZERO + Y + k, X, stride=ROWS), :] = right_ref[Y_PERT + k]
    for c, b in enumerate((0, 1, 2, 6, 7, 8)):
        for x in range(X):
            new[c, pl.ds((x + 1) * ROWS + ZERO, Y), :] = base_ref[b, pl.ds(x * Y, Y), :]
        new[c, pl.ds(ROWS + ZERO - 1, X, stride=ROWS), :] = left_ref[Y_BASE + c]
        new[c, pl.ds(ROWS + ZERO + Y, X, stride=ROWS), :] = right_ref[Y_BASE + c]
    odd = index_x % 2 == 1
    for ref, high in ((xa_ref, jnp.logical_not(odd)), (xb_ref, odd)):
        for d in (1, 2, 3):
            x = jnp.where(high, X - 1 + d, -d)
            rows = Y + 2 * (3 - d)
            for c in range(9):
                wide[c, pl.ds((x + 3) * ROWS + ZERO - (3 - d), rows), :] = ref[
                    pl.ds(now_row(c, d), rows), :
                ]
            if d < 3:
                pert[pl.ds((x + 2) * ROWS + ZERO - (2 - d), rows - 2), :] = ref[
                    pl.ds(pert_row(d), rows - 2), :
                ]
            if d == 1:
                for c in range(6):
                    new[c, pl.ds((x + 1) * ROWS + ZERO, Y), :] = ref[pl.ds(X_BASE + c * Y, Y), :]

    def row_mask(first, rows):
        y = lax.broadcasted_iota(jnp.int32, (rows, Z), 0) + first
        return ((y >= 0) | (index_y > 0)) & ((y < Y) | (index_y < last_y))

    def plane_valid(x):
        return ((x >= 0) | (index_x > 0)) & ((x < X) | (index_x < last_x))

    def along_z(value):
        lane = lax.broadcasted_iota(jnp.int32, value.shape, 1)
        after = jnp.where(lane < Z - 1, pltpu.roll(value, Z - 1, 1), 0.0)
        before = jnp.where(lane > 0, pltpu.roll(value, 1, 1), 0.0)
        return after - before

    def differences(ref, c, row, rows):
        return (
            ref[c, pl.ds(row + ROWS, rows), :] - ref[c, pl.ds(row - ROWS, rows), :],
            ref[c, pl.ds(row + 1, rows), :] - ref[c, pl.ds(row - 1, rows), :],
            along_z(ref[c, pl.ds(row, rows), :]),
        )

    wide_mask = row_mask(-2, 24)
    lame_rows = jnp.where(wide_mask, 0.5 * lame_ref[...].reshape(1, Z), 0.0)
    shear_rows = jnp.where(wide_mask, shear_ref[...].reshape(1, Z), 0.0)

    @pl.loop(-2, X + 2)
    def _(x):
        row = (x + 3) * ROWS + ZERO - 2
        out = (x + 2) * ROWS + ZERO - 2
        valid = plane_valid(x)
        lame = jnp.where(valid, lame_rows, 0.0)
        shear = jnp.where(valid, shear_rows, 0.0)
        half_shear = 0.5 * shear
        moved = pert[pl.ds(out, 24), :]
        half_moved = 0.5 * moved
        first = None
        for field in range(3):
            gx, gy, gz = zip(*[differences(wide, 3 * field + i, row, 24) for i in range(3)])
            normal = (gx[0], gy[1], gz[2])
            skew = (gy[0] + gx[1], gz[0] + gx[2], gz[1] + gy[2])
            if field == 0:
                first = (normal, skew)
            volume = lame * (gx[0] + gy[1] + gz[2])
            for i in range(3):
                total = shear * normal[i] + volume
                if field == 1:
                    total = total + moved * first[0][i]
                stress[6 * field + i, pl.ds(out, 24), :] = total
                total = half_shear * skew[i]
                if field == 1:
                    total = total + half_moved * first[1][i]
                stress[6 * field + 3 + i, pl.ds(out, 24), :] = total

    new_mask = row_mask(-1, 24)
    scale_rows = jnp.where(new_mask, 0.05 * buoy_ref[...].reshape(1, Z), 0.0)
    top = lax.broadcasted_iota(jnp.int32, (24, Z), 1) == 0
    received_rows = jnp.where(top, 0.1 * buoy_ref[...].reshape(1, Z), 0.0)

    @pl.loop(-1, X + 1)
    def _(x):
        row = (x + 2) * ROWS + ZERO - 1
        out = (x + 1) * ROWS + ZERO - 1
        scale = jnp.where(plane_valid(x), scale_rows, 0.0)

        def across_x(c):
            return stress[c, pl.ds(row + ROWS, 24), :] - stress[c, pl.ds(row - ROWS, 24), :]

        def across_y(c):
            return stress[c, pl.ds(row + 1, 24), :] - stress[c, pl.ds(row - 1, 24), :]

        def across_z(c):
            return along_z(stress[c, pl.ds(row, 24), :])

        change = []
        for field in range(3):
            o = 6 * field
            change.append(
                (
                    scale * (across_x(o) + across_y(o + 3) + across_z(o + 4)),
                    scale * (across_x(o + 3) + across_y(o + 1) + across_z(o + 5)),
                    scale * (across_x(o + 4) + across_y(o + 5) + across_z(o + 2)),
                )
            )
        for i in range(3):
            new[i, pl.ds(out, 24), :] = new[i, pl.ds(out, 24), :] + change[0][i]
            new[3 + i, pl.ds(out, 24), :] = new[3 + i, pl.ds(out, 24), :] + (
                change[2][i] + received_rows * change[1][i]
            )

        @pl.when((x >= 0) & (x < X))
        def _():
            at = pl.multiple_of(x * Y, Y)
            for i in range(3):
                bnext_ref[i, pl.ds(at, Y), :] = (
                    base_ref[3 + i, pl.ds(at, Y), :] + change[1][i][1 : Y + 1]
                )

    @pl.loop(0, X)
    def _(x):
        row = pl.multiple_of((x + 1) * ROWS + ZERO, 8)
        at = pl.multiple_of(x * Y, Y)
        for i in range(3):
            fnext_ref[i, pl.ds(at, Y), :] = new[i, pl.ds(row, Y), :]
            aprev_ref[i, pl.ds(at, Y), :] = new[3 + i, pl.ds(row, Y), :]
        hx, hy, hz = zip(*[differences(new, i, row, Y) for i in range(3)])
        kx, ky, kz = zip(*[differences(new, 3 + i, row, Y) for i in range(3)])
        normal = hx[0] * kx[0] + hy[1] * ky[1] + hz[2] * kz[2]
        skew = (
            (hy[0] + hx[1]) * (ky[0] + kx[1])
            + (hz[0] + hx[2]) * (kz[0] + kx[2])
            + (hz[1] + hy[2]) * (kz[1] + ky[2])
        )
        hess_ref[pl.ds(at, Y), :] = -0.0125 * (2.0 * normal + skew)


def shape(*dims):
    return jax.ShapeDtypeStruct(dims, F32)


HBM = pl.BlockSpec(memory_space=pltpu.HBM)
VMEM = pl.BlockSpec(memory_space=pltpu.VMEM)
SMEM = pl.BlockSpec(memory_space=pltpu.SMEM)


def on_device(
    forward_prev,
    forward_now,
    born_prev,
    born_now,
    adjoint_now,
    adjoint_next,
    shear_pert,
    lame_depth,
    shear_depth,
    buoyancy,
    drm_cells,
    drm_matrix,
    drm_motion,
    source_cell,
    source_force,
):
    assert forward_now.shape == (1, 3, X, Y, Z)
    count_x = lax.axis_size("gx")
    count_y = lax.axis_size("gy")
    events = lax.axis_size("event")
    place = jnp.stack(
        [
            lax.axis_index("gx"),
            lax.axis_index("gy"),
            jnp.int32(count_y * Y),
            jnp.int32(count_x),
            jnp.int32(count_y),
        ]
    ).astype(jnp.int32)
    flat = [
        a.reshape(3, CELLS, Z)
        for a in (forward_prev, forward_now, born_prev, born_now, adjoint_now, adjoint_next)
    ]
    pert = shear_pert.reshape(CELLS, Z)
    lame, shear, buoy = (a.reshape(1, Z) for a in (lame_depth, shear_depth, buoyancy))

    begin_inputs = (
        *flat,
        pert,
        buoy,
        drm_cells.reshape(1, ELEMS),
        drm_matrix.reshape(9, 1, ELEMS),
        drm_motion.reshape(3, 1, ELEMS),
        source_cell,
        source_force,
    )
    base, low, high, xa, xb = pl.pallas_call(
        begin_kernel,
        out_shape=(
            shape(9, CELLS, Z),
            shape(Y_PLANES, X, Z),
            shape(Y_PLANES, X, Z),
            shape(X_ROWS, Z),
            shape(X_ROWS, Z),
        ),
        in_specs=[SMEM] + [HBM] * 13,
        out_specs=[VMEM] * 5,
        scratch_shapes=[pltpu.VMEM((3, CELLS, Z), F32)]
        + [pltpu.VMEM(a.shape, a.dtype) for a in begin_inputs[:11]]
        + [pltpu.SMEM((1,), jnp.int32), pltpu.VMEM((1, 3), F32)]
        + [pltpu.SemaphoreType.DMA((13,))],
        compiler_params=pltpu.CompilerParams(vmem_limit_bytes=60 * 2**20),
        name="begin",
    )(
        place,
        *begin_inputs,
    )

    left = lax.ppermute(high, "gy", [(i, i + 1) for i in range(count_y - 1)])
    right = lax.ppermute(low, "gy", [(i + 1, i) for i in range(count_y - 1)])

    xa, xb = pl.pallas_call(
        widen_kernel,
        out_shape=(shape(X_ROWS, Z), shape(X_ROWS, Z)),
        in_specs=[SMEM] + [VMEM] * 4,
        out_specs=[VMEM] * 2,
        compiler_params=pltpu.CompilerParams(vmem_limit_bytes=16 * 2**20),
        name="widen",
    )(place, xa, xb, left, right)

    def swap(first):
        pairs = []
        for i in range(first, count_x - 1, 2):
            pairs += [(i, i + 1), (i + 1, i)]
        return pairs

    xa = lax.ppermute(xa, "gx", swap(0))
    xb = lax.ppermute(xb, "gx", swap(1))

    hess, forward_next, born_next, adjoint_prev = pl.pallas_call(
        step_kernel,
        out_shape=(shape(CELLS, Z), shape(3, CELLS, Z), shape(3, CELLS, Z), shape(3, CELLS, Z)),
        in_specs=[SMEM] + [VMEM] * 12,
        out_specs=[VMEM] * 4,
        scratch_shapes=[
            pltpu.VMEM((9, (X + 6) * ROWS, Z), F32),
            pltpu.VMEM(((X + 4) * ROWS, Z), F32),
            pltpu.VMEM((18, (X + 4) * ROWS, Z), F32),
            pltpu.VMEM((6, (X + 2) * ROWS, Z), F32),
        ],
        compiler_params=pltpu.CompilerParams(vmem_limit_bytes=36 * 2**20),
        name="step",
    )(
        place,
        flat[1],
        flat[3],
        flat[4],
        pert,
        base,
        left,
        right,
        xa,
        xb,
        lame,
        shear,
        buoy,
    )

    parts = lax.all_to_all(hess.reshape(events, CELLS // events, Z), "event", 0, 0, tiled=True)
    part = jnp.sum(parts, axis=0)
    spread = jnp.broadcast_to(part[None], (events, CELLS // events, Z))
    hess = lax.all_to_all(spread, "event", 0, 0, tiled=True)

    whole = (1, 3, X, Y, Z)
    return (
        hess.reshape(X, Y, Z),
        forward_next.reshape(whole),
        born_next.reshape(whole),
        adjoint_prev.reshape(whole),
    )


def solution(mesh):
    field = P("event", None, "gx", "gy", None)
    return jax.shard_map(
        on_device,
        mesh=mesh,
        in_specs=(field,) * 6
        + (
            P("gx", "gy", None),
            P(),
            P(),
            P(),
            P("gx", "gy", None),
            P(None, None, "gx", "gy", None),
            P("event", None, "gx", "gy", None),
            P("event"),
            P("event", None),
        ),
        out_specs=(P("gx", "gy", None), field, field, field),
        check_vma=False,
    )
```

time: 303 us -> 79.7 us (0.26)
  the two profiles are of different devices: /device:TPU:30 before, /device:TPU:200 now
where the time goes in v1:
time: 79.7 us; the launch traced here: 79.3 us
  blocking collectives  32.3 us (41%)
  waiting for transfers between devices  15.5 us (19%)
  Pallas kernels  13.5 us (17%)
  starting transfers between devices  11.9 us (15%)
  local copies, waits for them, and re-layouts  4.57 us (6%)
  between operations  1.44 us (2%)
    all_to_all x1, blocking collectives, on_device(): lax.all_to_all(hess.reshape(events, CELLS // events, Z), 'event', 0, 0, t...  18.9 us
    all_to_all x1, blocking collectives, on_device(): hess = lax.all_to_all(spread, 'event', 0, 0, tiled=True)  13.5 us
    pallas_call x1, Pallas kernels, on_device(): pl.pallas_call(step_kernel, out_shape=(shape(CELLS, Z), shape(3, CELLS, Z...  8.68 us
    ppermute x1, waiting for transfers between devices, on_device(): xb = lax.ppermute(xb, 'gx', swap(1))  5.78 us
    ppermute x1, starting transfers between devices, on_device(): left = lax.ppermute(high, 'gy', [(i, i + 1) for i in range(count_y - 1)])  5.62 us
    ppermute x1, waiting for transfers between devices, on_device(): right = lax.ppermute(low, 'gy', [(i + 1, i) for i in range(count_y - 1)])  5.22 us
    ppermute x1, waiting for transfers between devices, on_device(): left = lax.ppermute(high, 'gy', [(i, i + 1) for i in range(count_y - 1)])  4.46 us
    pallas_call x1, Pallas kernels, on_device(): pl.pallas_call(begin_kernel, out_shape=(shape(9, CELLS, Z), shape(Y_PLANE...  4.24 us
  transfers between devices with their start and end apart: 4, of which 3 were waited for; matrix products, arithmetic and copies ran while one was open for 0% of the time, Pallas kernels for 0%

profile of v1, /device:TPU:200, one launch (start us, length us, event | category | flops | bytes accessed | tf_op | source)
XLA Modules:
  0.0 79.3 jit_solution(16861631096827889950)
XLA Ops:
  1.3 0.7 stack.11.place_ref
  2.0 0.0 copy-start.7
  2.0 0.0 copy-start.4
  2.0 0.0 copy-start.8
  2.0 0.0 copy-start.9
  2.0 0.0 copy-start.10
  2.0 4.2 %begin.1 = (f32[9,256,128]{2,1,0:T(8,128)}, f32[35,16,128]{2,1,0:T(8,128)}, f32[35,16,128]{2,1,0:T(8,128)}, f32[616,128]{1,0:T(8,128)}, f32[616,128]{1,0:T(8,128)}) custom-call(s32[5]{0:T(128)} %stack.11.place_ref, f32[3,256,128]{2,1,0:T(8,128)} %bitcast.32, f32[3,256,128]{2,1,0:T(8,128)} %bitcast.19, f32[3,256,128]{2,1,0:T(8,128)} %bitcast.33, ...), custom_call_target="tpu_custom_call" | custom-call | tf_op jit(solution)/shard_map/begin/pallas_call | solution.py:396
  6.2 0.0 copy-start
  6.2 0.0 copy-start.1
  6.2 0.0 copy-start.2
  6.3 5.6 %collective-permute-start = (f32[35,16,128]{2,1,0:T(8,128)}, f32[35,16,128]{2,1,0:T(8,128)S(1)}, u32[]{:S(2)}, u32[]{:S(2)}) collective-permute-start(f32[35,16,128]{2,1,0:T(8,128)} %get-tuple-element.16), channel_id=1, source_target_pairs={{0,1},{1,2},{2,3},{3,4},{4,5},{5,6},{6,7},{7,8},{8,9},{9,10},{10,1... | collective-permute-start | bytes 860168 | tf_op jit(solution)/shard_map/ppermute | solution.py:418
  11.9 1.9 %collective-permute-start.1 = (f32[35,16,128]{2,1,0:T(8,128)}, f32[35,16,128]{2,1,0:T(8,128)S(1)}, u32[]{:S(2)}, u32[]{:S(2)}) collective-permute-start(f32[35,16,128]{2,1,0:T(8,128)} %get-tuple-element.17), channel_id=1, source_target_pairs={{1,0},{2,1},{3,2},{4,3},{5,4},{6,5},{7,6},{8,7},{9,8},{10,9},{11,1... | collective-permute-start | bytes 860168 | tf_op jit(solution)/shard_map/ppermute | solution.py:419
  13.8 4.5 %collective-permute-done.left_ref = f32[35,16,128]{2,1,0:T(8,128)S(1)} collective-permute-done((f32[35,16,128]{2,1,0:T(8,128)}, f32[35,16,128]{2,1,0:T(8,128)S(1)}, u32[]{:S(2)}, u32[]{:S(2)}) %collective-permute-start) | collective-permute-done | bytes 286752 | tf_op jit(solution)/shard_map/ppermute | solution.py:418
  18.3 5.2 %collective-permute-done.1.right_ref = f32[35,16,128]{2,1,0:T(8,128)S(1)} collective-permute-done((f32[35,16,128]{2,1,0:T(8,128)}, f32[35,16,128]{2,1,0:T(8,128)S(1)}, u32[]{:S(2)}, u32[]{:S(2)}) %collective-permute-start.1) | collective-permute-done | bytes 286752 | tf_op jit(solution)/shard_map/ppermute | solution.py:419
  23.5 0.0 copy-done.7
  23.5 0.0 copy-start.5
  23.5 1.0 %copy-done.5 = f32[616,128]{1,0:T(8,128)S(1)} copy-done((f32[616,128]{1,0:T(8,128)S(1)}, f32[616,128]{1,0:T(8,128)}, u32[]{:S(2)}) %copy-start.5) | copy-done | bytes 315416
  24.5 0.0 copy-start.6
  24.5 1.0 %copy-done.6 = f32[616,128]{1,0:T(8,128)S(1)} copy-done((f32[616,128]{1,0:T(8,128)S(1)}, f32[616,128]{1,0:T(8,128)}, u32[]{:S(2)}) %copy-start.6) | copy-done | bytes 315416
  25.4 0.6 widen.1
  26.1 1.9 %collective-permute-start.2 = (f32[616,128]{1,0:T(8,128)S(1)}, f32[616,128]{1,0:T(8,128)S(1)}, u32[]{:S(2)}, u32[]{:S(2)}) collective-permute-start(f32[616,128]{1,0:T(8,128)S(1)} %get-tuple-element.20), channel_id=1, source_target_pairs={{0,12},{12,0},{24,36},{36,24},{1,13},{13,1},{25,37},{37,25},{2,14}... | collective-permute-start | bytes 946184 | tf_op jit(solution)/shard_map/ppermute | solution.py:436
  28.0 2.5 %collective-permute-start.3 = (f32[616,128]{1,0:T(8,128)S(1)}, f32[616,128]{1,0:T(8,128)S(1)}, u32[]{:S(2)}, u32[]{:S(2)}) collective-permute-start(f32[616,128]{1,0:T(8,128)S(1)} %get-tuple-element.21), channel_id=1, source_target_pairs={{12,24},{24,12},{13,25},{25,13},{14,26},{26,14},{15,27},{27,15},{1... | collective-permute-start | bytes 946184 | tf_op jit(solution)/shard_map/ppermute | solution.py:437
  30.5 0.0 collective-permute-done.2.xa_ref
  30.5 5.8 %collective-permute-done.3.xb_ref = f32[616,128]{1,0:T(8,128)S(1)} collective-permute-done((f32[616,128]{1,0:T(8,128)S(1)}, f32[616,128]{1,0:T(8,128)S(1)}, u32[]{:S(2)}, u32[]{:S(2)}) %collective-permute-start.3) | collective-permute-done | bytes 315424 | tf_op jit(solution)/shard_map/ppermute | solution.py:437
  36.3 0.0 copy-done.4
  36.3 0.0 copy-done.8
  36.3 0.0 copy-done.9
  36.3 0.0 copy-done.10
  36.3 0.0 copy-done
  36.3 0.0 copy-done.1
  36.3 0.0 copy-done.2
  36.3 0.0 copy-start.3
  36.3 1.3 %copy-done.3 = f32[9,256,128]{2,1,0:T(8,128)S(1)} copy-done((f32[9,256,128]{2,1,0:T(8,128)S(1)}, f32[9,256,128]{2,1,0:T(8,128)}, u32[]{:S(2)}) %copy-start.3) | copy-done | bytes 1179672
  37.6 8.7 %step.1 = (f32[256,128]{1,0:T(8,128)S(1)}, f32[3,256,128]{2,1,0:T(8,128)}, f32[3,256,128]{2,1,0:T(8,128)}, f32[3,256,128]{2,1,0:T(8,128)}) custom-call(s32[5]{0:T(128)S(1)} %copy-done.7, f32[3,256,128]{2,1,0:T(8,128)S(1)} %bitcast.20, f32[3,256,128]{2,1,0:T(8,128)S(1)} %bitcast.22, f32[3,256,128]{2,1,0:T(8,128)S(1)} %bitcast.24, f32[256,128]{1,0:T(8,128)S(1)} %bitcast.26, ...), custom_call_target="tpu_custom_call" | custom-call | tf_op jit(solution)/shard_map/step/pallas_call | solution.py:439
  46.3 18.9 %all_to_all.10 = f32[16,16,128]{2,1,0:T(8,128)S(1)} all-to-all(f32[16,16,128]{2,1,0:T(8,128)S(1)} %bitcast.27), channel_id=1, replica_groups=mesh['event'=16,'gx'=4,'gy'=12] {'event'}, dimensions={0} | all-to-all | bytes 262144 | tf_op jit(solution)/shard_map/all_to_all | solution.py:468
  65.2 13.5 %all_to_all.11 = f32[16,16,128]{2,1,0:T(8,128)S(1)} all-to-all(f32[16,16,128]{2,1,0:T(8,128)S(1)} %broadcast_in_dim.2), channel_id=1, replica_groups=mesh['event'=16,'gx'=4,'gy'=12] {'event'}, dimensions={0} | all-to-all | bytes 262144 | tf_op jit(solution)/shard_map/all_to_all | solution.py:471
  78.6 0.7 copy.21
  (2 shorter events, 0.0 us)
Async XLA Ops:
  2.0 21.5 %copy-start.7 = (s32[5]{0:T(128)S(1)}, s32[5]{0:T(128)}, u32[]{:S(2)}) copy-start(s32[5]{0:T(128)} %stack.11.place_ref) | copy-start | bytes 64
  2.0 34.3 %copy-start.4 = (f32[16,16,128]{2,1,0:T(8,128)S(1)}, f32[16,16,128]{2,1,0:T(8,128)}, u32[]{:S(2)}) copy-start(f32[16,16,128]{2,1,0:T(8,128)} %param.21) | copy-start | bytes 393220
  2.0 34.3 %copy-start.8 = (f32[128]{0:T(128)S(1)}, f32[128]{0:T(128)}, u32[]{:S(2)}) copy-start(f32[128]{0:T(128)} %param.24) | copy-start | bytes 1540
  2.0 34.3 %copy-start.9 = (f32[128]{0:T(128)S(1)}, f32[128]{0:T(128)}, u32[]{:S(2)}) copy-start(f32[128]{0:T(128)} %param.22) | copy-start | bytes 1540
  2.0 34.3 %copy-start.10 = (f32[128]{0:T(128)S(1)}, f32[128]{0:T(128)}, u32[]{:S(2)}) copy-start(f32[128]{0:T(128)} %param.23) | copy-start | bytes 1540
  6.2 30.1 %copy-start = (f32[1,3,16,16,128]{4,3,2,1,0:T(8,128)S(1)}, f32[1,3,16,16,128]{4,3,2,1,0:T(8,128)}, u32[]{:S(2)}) copy-start(f32[1,3,16,16,128]{4,3,2,1,0:T(8,128)} %param.16) | copy-start | bytes 1179652
  6.2 30.1 %copy-start.1 = (f32[1,3,16,16,128]{4,3,2,1,0:T(8,128)S(1)}, f32[1,3,16,16,128]{4,3,2,1,0:T(8,128)}, u32[]{:S(2)}) copy-start(f32[1,3,16,16,128]{4,3,2,1,0:T(8,128)} %param.18) | copy-start | bytes 1179652
  6.2 30.1 %copy-start.2 = (f32[1,3,16,16,128]{4,3,2,1,0:T(8,128)S(1)}, f32[1,3,16,16,128]{4,3,2,1,0:T(8,128)}, u32[]{:S(2)}) copy-start(f32[1,3,16,16,128]{4,3,2,1,0:T(8,128)} %param.19) | copy-start | bytes 1179652
  6.3 12.0 %collective-permute-start = (f32[35,16,128]{2,1,0:T(8,128)}, f32[35,16,128]{2,1,0:T(8,128)S(1)}, u32[]{:S(2)}, u32[]{:S(2)}) collective-permute-start(f32[35,16,128]{2,1,0:T(8,128)} %get-tuple-element.16), channel_id=1, source_target_pairs={{0,1},{1,2},{2,3},{3,4},{4,5},{5,6},{6,7},{7,8},{8,9},{9,10},{10,1... | collective-permute-start | bytes 860168 | tf_op jit(solution)/shard_map/ppermute | solution.py:418
  11.9 11.6 %collective-permute-start.1 = (f32[35,16,128]{2,1,0:T(8,128)}, f32[35,16,128]{2,1,0:T(8,128)S(1)}, u32[]{:S(2)}, u32[]{:S(2)}) collective-permute-start(f32[35,16,128]{2,1,0:T(8,128)} %get-tuple-element.17), channel_id=1, source_target_pairs={{1,0},{2,1},{3,2},{4,3},{5,4},{6,5},{7,6},{8,7},{9,8},{10,9},{11,1... | collective-permute-start | bytes 860168 | tf_op jit(solution)/shard_map/ppermute | solution.py:419
  23.5 1.0 %copy-start.5 = (f32[616,128]{1,0:T(8,128)S(1)}, f32[616,128]{1,0:T(8,128)}, u32[]{:S(2)}) copy-start(f32[616,128]{1,0:T(8,128)} %get-tuple-element.18.xa_in) | copy-start | bytes 946180
  24.5 1.0 %copy-start.6 = (f32[616,128]{1,0:T(8,128)S(1)}, f32[616,128]{1,0:T(8,128)}, u32[]{:S(2)}) copy-start(f32[616,128]{1,0:T(8,128)} %get-tuple-element.19.xb_in) | copy-start | bytes 946180
  26.1 4.4 %collective-permute-start.2 = (f32[616,128]{1,0:T(8,128)S(1)}, f32[616,128]{1,0:T(8,128)S(1)}, u32[]{:S(2)}, u32[]{:S(2)}) collective-permute-start(f32[616,128]{1,0:T(8,128)S(1)} %get-tuple-element.20), channel_id=1, source_target_pairs={{0,12},{12,0},{24,36},{36,24},{1,13},{13,1},{25,37},{37,25},{2,14}... | collective-permute-start | bytes 946184 | tf_op jit(solution)/shard_map/ppermute | solution.py:436
  28.0 8.3 %collective-permute-start.3 = (f32[616,128]{1,0:T(8,128)S(1)}, f32[616,128]{1,0:T(8,128)S(1)}, u32[]{:S(2)}, u32[]{:S(2)}) collective-permute-start(f32[616,128]{1,0:T(8,128)S(1)} %get-tuple-element.21), channel_id=1, source_target_pairs={{12,24},{24,12},{13,25},{25,13},{14,26},{26,14},{15,27},{27,15},{1... | collective-permute-start | bytes 946184 | tf_op jit(solution)/shard_map/ppermute | solution.py:437
  36.3 1.3 %copy-start.3 = (f32[9,256,128]{2,1,0:T(8,128)S(1)}, f32[9,256,128]{2,1,0:T(8,128)}, u32[]{:S(2)}) copy-start(f32[9,256,128]{2,1,0:T(8,128)} %get-tuple-element.15.base_ref) | copy-start | bytes 3538948

commit v2 on v1

--- a/solution.py
+++ b/solution.py
@@ -1,3 +1,5 @@
+import functools
+
 import jax
 import jax.numpy as jnp
 from jax import lax
@@ -39,34 +41,7 @@
     return jnp.where(high, X - d, d - 1)
 
 
-def begin_kernel(
-    place_ref,
-    *refs,
-):
-    sources, refs = refs[:13], refs[13:]
-    base_ref, low_ref, high_ref, xa_ref, xb_ref, applied_ref = refs[:6]
-    held, arrived = refs[6:19], refs[19]
-    copies = [
-        pltpu.make_async_copy(source, ref, arrived.at[i])
-        for i, (source, ref) in enumerate(zip(sources, held))
-    ]
-    for i in (8, 9, 10, 11, 12, 7, 6, 0, 1, 2, 3, 4, 5):
-        copies[i].start()
-    fprev_ref, fnow_ref, bprev_ref, bnow_ref, anow_ref, anext_ref = held[:6]
-    pert_ref, buoy_ref, cells_ref, matrix_ref, motion_ref, cell_ref, force_ref = held[6:]
-    for i in (8, 9, 10, 11, 12):
-        copies[i].wait()
-
-    index_x = place_ref[0]
-    index_y = place_ref[1]
-    total_y = place_ref[2]
-
-    cells = cells_ref[...].reshape(1, ELEMS)
-    column = cells // Z
-    depth = cells % Z
-    pick = jnp.where(
-        lax.broadcasted_iota(jnp.int32, (CELLS, ELEMS), 0) == column, 1.0, 0.0
-    ).astype(jnp.bfloat16)
+def element_force(depth, matrix_ref, motion_ref):
     slot = lax.broadcasted_iota(jnp.int32, (16, ELEMS), 0)
     spread = jnp.zeros((16, ELEMS), F32)
     for i in range(3):
@@ -75,61 +50,115 @@
             for c in range(3)
         )
         spread = jnp.where(slot == depth - (Z - 16) - 4 * i, element, spread)
-    spread = jnp.concatenate([jnp.zeros((Z - 16, ELEMS), F32), spread], axis=0)
-    placed = jnp.zeros((CELLS, Z), F32)
-    rest = spread
+    rest = jnp.concatenate([jnp.zeros((Z - 16, ELEMS), F32), spread], axis=0)
+    parts = []
     for _ in range(3):
-        part = rest.astype(jnp.bfloat16)
+        parts.append(rest.astype(jnp.bfloat16))
+        rest = rest - parts[-1].astype(F32)
+    return parts
+
+
+def placed_force(columns, cells_ref, matrix_ref, motion_ref):
+    rows = columns.shape[0]
+    cells = cells_ref[...].reshape(1, ELEMS)
+    pick = jnp.where(columns == cells // Z, 1.0, 0.0).astype(jnp.bfloat16)
+    placed = jnp.zeros((rows, Z), F32)
+    for part in element_force(cells % Z, matrix_ref, motion_ref):
         placed = placed + lax.dot_general(
             pick, part, (((1,), (1,)), ((), ())), preferred_element_type=F32
         )
-        rest = rest - part.astype(F32)
-    lane = lax.broadcasted_iota(jnp.int32, (CELLS, Z), 1)
+    lane = lax.broadcasted_iota(jnp.int32, (rows, Z), 1)
+    applied = []
     for i in range(3):
         moved = placed if i == 0 else pltpu.roll(placed, 4 * i, 1)
-        applied_ref[i] = jnp.where(lane >= Z - LAYER, moved, 0.0)
-
-    cell = cell_ref[0]
-    local_x = cell // (total_y * Z) - index_x * X
-    local_y = (cell // Z) % total_y - index_y * Y
-    inside = (local_x >= 0) & (local_x < X) & (local_y >= 0) & (local_y < Y)
-
-    @pl.when(inside)
-    def _():
-        row = local_x * Y + local_y
-        here = lax.broadcasted_iota(jnp.int32, (1, Z), 1) == cell % Z
-        for i in range(3):
-            old = applied_ref[i, pl.ds(row, 1), :]
-            applied_ref[i, pl.ds(row, 1), :] = old + jnp.where(here, force_ref[:, i : i + 1], 0.0)
-
-    for i in (7, 6, 0, 1, 2, 3, 4, 5):
+        applied.append(jnp.where(lane >= Z - LAYER, moved, 0.0))
+    return applied
+
+
+def plane_rows(ref, y):
+    return ref[pl.ds(y, X, stride=Y), :]
+
+
+def begin_kernel(*refs):
+    sources, low_ref, high_ref = refs[:11], refs[11], refs[12]
+    held, arrived = refs[13:24], refs[24]
+    copies = [
+        pltpu.make_async_copy(source, ref, arrived.at[i])
+        for i, (source, ref) in enumerate(zip(sources, held))
+    ]
+    order = (8, 9, 10, 1, 3, 4, 6, 7, 0, 2, 5)
+    for i in order:
+        copies[i].start()
+    fprev_ref, fnow_ref, bprev_ref, bnow_ref, anow_ref, anext_ref = held[:6]
+    pert_ref, buoy_ref, cells_ref, matrix_ref, motion_ref = held[6:]
+    for i in order[:3]:
+        copies[i].wait()
+
+    row = lax.broadcasted_iota(jnp.int32, (2 * X, ELEMS), 0)
+    columns = (row % X) * Y + jnp.where(row < X, 0, Y - 1)
+    applied = placed_force(columns, cells_ref, matrix_ref, motion_ref)
+
+    for i in order[3:7]:
+        copies[i].wait()
+    now = [r.at[i] for r in (fnow_ref, bnow_ref, anow_ref) for i in range(3)]
+    for c in range(9):
+        for k in range(3):
+            low_ref[3 * c + k] = plane_rows(now[c], k)
+            high_ref[3 * c + k] = plane_rows(now[c], Y - 3 + k)
+    for k in range(2):
+        low_ref[Y_PERT + k] = plane_rows(pert_ref, k)
+        high_ref[Y_PERT + k] = plane_rows(pert_ref, Y - 2 + k)
+
+    for i in order[7:]:
         copies[i].wait()
     scale = 0.1 * buoy_ref[...].reshape(1, Z)
-    surface_scale = jnp.where(lane[:1] == 0, scale, 0.0)
+    top = lax.broadcasted_iota(jnp.int32, (1, Z), 1) == 0
+    surface_scale = jnp.where(top, scale, 0.0)
+    for ref, y, first in ((low_ref, 0, 0), (high_ref, Y - 1, X)):
+        for i in range(3):
+            ref[Y_BASE + i] = (
+                2.0 * plane_rows(now[i], y)
+                - plane_rows(fprev_ref.at[i], y)
+                + scale * applied[i][first : first + X]
+            )
+            born = 2.0 * plane_rows(now[3 + i], y) - plane_rows(bprev_ref.at[i], y)
+            ref[Y_BASE + 3 + i] = (
+                2.0 * plane_rows(now[6 + i], y)
+                - plane_rows(anext_ref.at[i], y)
+                + surface_scale * born
+            )
+
+
+def base_kernel(
+    fprev_ref,
+    fnow_ref,
+    bprev_ref,
+    bnow_ref,
+    anow_ref,
+    anext_ref,
+    pert_ref,
+    buoy_ref,
+    cells_ref,
+    matrix_ref,
+    motion_ref,
+    base_ref,
+    xa_ref,
+    xb_ref,
+):
+    columns = lax.broadcasted_iota(jnp.int32, (CELLS, ELEMS), 0)
+    applied = placed_force(columns, cells_ref, matrix_ref, motion_ref)
+    scale = 0.1 * buoy_ref[...].reshape(1, Z)
+    top = lax.broadcasted_iota(jnp.int32, (1, Z), 1) == 0
+    surface_scale = jnp.where(top, scale, 0.0)
     for i in range(3):
-        base_ref[i] = 2.0 * fnow_ref[i] - fprev_ref[i] + scale * applied_ref[i]
+        base_ref[i] = 2.0 * fnow_ref[i] - fprev_ref[i] + scale * applied[i]
         born = 2.0 * bnow_ref[i] - bprev_ref[i]
         base_ref[3 + i] = born
         base_ref[6 + i] = 2.0 * anow_ref[i] - anext_ref[i] + surface_scale * born
 
     now = [r.at[i] for r in (fnow_ref, bnow_ref, anow_ref) for i in range(3)]
     bases = [base_ref.at[i] for i in (0, 1, 2, 6, 7, 8)]
-
-    def column_of(ref, y):
-        return ref[pl.ds(y, X, stride=Y), :]
-
-    for c in range(9):
-        for k in range(3):
-            low_ref[3 * c + k] = column_of(now[c], k)
-            high_ref[3 * c + k] = column_of(now[c], Y - 3 + k)
-    for c in range(6):
-        low_ref[Y_BASE + c] = column_of(bases[c], 0)
-        high_ref[Y_BASE + c] = column_of(bases[c], Y - 1)
-    for k in range(2):
-        low_ref[Y_PERT + k] = column_of(pert_ref, k)
-        high_ref[Y_PERT + k] = column_of(pert_ref, Y - 2 + k)
-
-    odd = index_x % 2 == 1
+    odd = lax.axis_index("gx") % 2 == 1
     for ref, high in ((xa_ref, jnp.logical_not(odd)), (xb_ref, odd)):
 
         def plane_of(source, d):
@@ -145,8 +174,8 @@
             ref[pl.ds(X_BASE + c * Y, Y), :] = plane_of(bases[c], 1)
 
 
-def widen_kernel(place_ref, xa_in, xb_in, left_ref, right_ref, xa_ref, xb_ref):
-    odd = place_ref[0] % 2 == 1
+def widen_kernel(xa_in, xb_in, left_ref, right_ref, xa_ref, xb_ref):
+    odd = lax.axis_index("gx") % 2 == 1
     for source, ref, high in ((xa_in, xa_ref, jnp.logical_not(odd)), (xb_in, xb_ref, odd)):
         ref[...] = source[...]
         for d in (1, 2):
@@ -162,7 +191,8 @@
 
 
 def step_kernel(
-    place_ref,
+    count_x,
+    count_y,
     fnow_ref,
     bnow_ref,
     anow_ref,
@@ -175,6 +205,8 @@
     lame_ref,
     shear_ref,
     buoy_ref,
+    cell_ref,
+    force_ref,
     hess_ref,
     fnext_ref,
     bnext_ref,
@@ -184,10 +216,8 @@
     stress,
     new,
 ):
-    index_x = place_ref[0]
-    index_y = place_ref[1]
-    last_x = place_ref[3] - 1
-    last_y = place_ref[4] - 1
+    index_x, index_y = lax.axis_index("gx"), lax.axis_index("gy")
+    last_x, last_y = count_x - 1, count_y - 1
 
     now = [r.at[i] for r in (fnow_ref, bnow_ref, anow_ref) for i in range(3)]
     for c in range(9):
@@ -247,7 +277,7 @@
     lame_rows = jnp.where(wide_mask, 0.5 * lame_ref[...].reshape(1, Z), 0.0)
     shear_rows = jnp.where(wide_mask, shear_ref[...].reshape(1, Z), 0.0)
 
-    @pl.loop(-2, X + 2)
+    @pl.loop(-2, X + 2, unroll=X + 4)
     def _(x):
         row = (x + 3) * ROWS + ZERO - 2
         out = (x + 2) * ROWS + ZERO - 2
@@ -278,9 +308,13 @@
     new_mask = row_mask(-1, 24)
     scale_rows = jnp.where(new_mask, 0.05 * buoy_ref[...].reshape(1, Z), 0.0)
     top = lax.broadcasted_iota(jnp.int32, (24, Z), 1) == 0
-    received_rows = jnp.where(top, 0.1 * buoy_ref[...].reshape(1, Z), 0.0)
-
-    @pl.loop(-1, X + 1)
+    point_rows = jnp.where(new_mask, 0.1 * buoy_ref[...].reshape(1, Z), 0.0)
+    received_rows = jnp.where(top, point_rows, 0.0)
+    point = [point_rows * force_ref[:, i : i + 1] for i in range(3)]
+    first_cell = (index_y * Y - 1 + lax.broadcasted_iota(jnp.int32, (24, Z), 0)) * Z
+    source_row = cell_ref[...] - first_cell
+
+    @pl.loop(-1, X + 1, unroll=X + 2)
     def _(x):
         row = (x + 2) * ROWS + ZERO - 1
         out = (x + 1) * ROWS + ZERO - 1
@@ -305,8 +339,11 @@
                     scale * (across_x(o + 4) + across_y(o + 5) + across_z(o + 2)),
                 )
             )
+        here = source_row == (index_x * X + x) * (count_y * Y * Z)
         for i in range(3):
-            new[i, pl.ds(out, 24), :] = new[i, pl.ds(out, 24), :] + change[0][i]
+            new[i, pl.ds(out, 24), :] = new[i, pl.ds(out, 24), :] + (
+                change[0][i] + jnp.where(here, point[i], 0.0)
+            )
             new[3 + i, pl.ds(out, 24), :] = new[3 + i, pl.ds(out, 24), :] + (
                 change[2][i] + received_rows * change[1][i]
             )
@@ -319,7 +356,7 @@
                     base_ref[3 + i, pl.ds(at, Y), :] + change[1][i][1 : Y + 1]
                 )
 
-    @pl.loop(0, X)
+    @pl.loop(0, X, unroll=X)
     def _(x):
         row = pl.multiple_of((x + 1) * ROWS + ZERO, 8)
         at = pl.multiple_of(x * Y, Y)
@@ -343,7 +380,6 @@
 
 HBM = pl.BlockSpec(memory_space=pltpu.HBM)
 VMEM = pl.BlockSpec(memory_space=pltpu.VMEM)
-SMEM = pl.BlockSpec(memory_space=pltpu.SMEM)
 
 
 def on_device(
@@ -367,15 +403,6 @@
     count_x = lax.axis_size("gx")
     count_y = lax.axis_size("gy")
     events = lax.axis_size("event")
-    place = jnp.stack(
-        [
-            lax.axis_index("gx"),
-            lax.axis_index("gy"),
-            jnp.int32(count_y * Y),
-            jnp.int32(count_x),
-            jnp.int32(count_y),
-        ]
-    ).astype(jnp.int32)
     flat = [
         a.reshape(3, CELLS, Z)
         for a in (forward_prev, forward_now, born_prev, born_now, adjoint_now, adjoint_next)
@@ -390,42 +417,38 @@
         drm_cells.reshape(1, ELEMS),
         drm_matrix.reshape(9, 1, ELEMS),
         drm_motion.reshape(3, 1, ELEMS),
-        source_cell,
-        source_force,
     )
-    base, low, high, xa, xb = pl.pallas_call(
+    low, high = pl.pallas_call(
         begin_kernel,
-        out_shape=(
-            shape(9, CELLS, Z),
-            shape(Y_PLANES, X, Z),
-            shape(Y_PLANES, X, Z),
-            shape(X_ROWS, Z),
-            shape(X_ROWS, Z),
-        ),
-        in_specs=[SMEM] + [HBM] * 13,
-        out_specs=[VMEM] * 5,
-        scratch_shapes=[pltpu.VMEM((3, CELLS, Z), F32)]
-        + [pltpu.VMEM(a.shape, a.dtype) for a in begin_inputs[:11]]
-        + [pltpu.SMEM((1,), jnp.int32), pltpu.VMEM((1, 3), F32)]
-        + [pltpu.SemaphoreType.DMA((13,))],
+        out_shape=(shape(Y_PLANES, X, Z), shape(Y_PLANES, X, Z)),
+        in_specs=[HBM] * 11,
+        out_specs=[VMEM] * 2,
+        scratch_shapes=[pltpu.VMEM(a.shape, a.dtype) for a in begin_inputs]
+        + [pltpu.SemaphoreType.DMA((11,))],
         compiler_params=pltpu.CompilerParams(vmem_limit_bytes=60 * 2**20),
         name="begin",
-    )(
-        place,
-        *begin_inputs,
-    )
+    )(*begin_inputs)
 
     left = lax.ppermute(high, "gy", [(i, i + 1) for i in range(count_y - 1)])
     right = lax.ppermute(low, "gy", [(i + 1, i) for i in range(count_y - 1)])
+
+    base, xa, xb = pl.pallas_call(
+        base_kernel,
+        out_shape=(shape(9, CELLS, Z), shape(X_ROWS, Z), shape(X_ROWS, Z)),
+        in_specs=[VMEM] * 11,
+        out_specs=[VMEM] * 3,
+        compiler_params=pltpu.CompilerParams(vmem_limit_bytes=16 * 2**20),
+        name="base",
+    )(*begin_inputs)
 
     xa, xb = pl.pallas_call(
         widen_kernel,
         out_shape=(shape(X_ROWS, Z), shape(X_ROWS, Z)),
-        in_specs=[SMEM] + [VMEM] * 4,
+        in_specs=[VMEM] * 4,
         out_specs=[VMEM] * 2,
-        compiler_params=pltpu.CompilerParams(vmem_limit_bytes=16 * 2**20),
+        compiler_params=pltpu.CompilerParams(vmem_limit_bytes=4 * 2**20),
         name="widen",
-    )(place, xa, xb, left, right)
+    )(xa, xb, left, right)
 
     def swap(first):
         pairs = []
@@ -437,9 +460,9 @@
     xb = lax.ppermute(xb, "gx", swap(1))
 
     hess, forward_next, born_next, adjoint_prev = pl.pallas_call(
-        step_kernel,
+        functools.partial(step_kernel, count_x, count_y),
         out_shape=(shape(CELLS, Z), shape(3, CELLS, Z), shape(3, CELLS, Z), shape(3, CELLS, Z)),
-        in_specs=[SMEM] + [VMEM] * 12,
+        in_specs=[VMEM] * 14,
         out_specs=[VMEM] * 4,
         scratch_shapes=[
             pltpu.VMEM((9, (X + 6) * ROWS, Z), F32),
@@ -447,10 +470,9 @@
             pltpu.VMEM((18, (X + 4) * ROWS, Z), F32),
             pltpu.VMEM((6, (X + 2) * ROWS, Z), F32),
         ],
-        compiler_params=pltpu.CompilerParams(vmem_limit_bytes=36 * 2**20),
+        compiler_params=pltpu.CompilerParams(vmem_limit_bytes=20 * 2**20),
         name="step",
     )(
-        place,
         flat[1],
         flat[3],
         flat[4],
@@ -463,6 +485,8 @@
         lame,
         shear,
         buoy,
+        source_cell[:, None] - lax.broadcasted_iota(jnp.int32, (1, Z), 1),
+        source_force,
     )
 
     parts = lax.all_to_all(hess.reshape(events, CELLS // events, Z), "event", 0, 0, tiled=True)

time: 79.7 us -> 68.3 us (0.86)
  Pallas kernels: 13.5 us -> 7.72 us
  local copies, waits for them, and re-layouts: 4.57 us -> 0.73 us
  waiting for transfers between devices: 15.5 us -> 13.8 us
    pallas_call x2 -> x3, Pallas kernels: 12.9 us -> 7.64 us  [the longest x1 4.05 us: on_device(): pl.pallas_call(functools.partial(step_kernel, count_x, count_y), out_shap...]
    unnamed x23 -> x29, local copies, waits for them, and re-layouts: 3.9 us -> 0.72 us
    ppermute x1, waiting for transfers between devices: 4.46 us -> 3.5 us  [on_device(): left = lax.ppermute(high, 'gy', [(i, i + 1) for i in range(count_y - 1)])]
  transfers between devices with their start and end apart: 4 -> 4, of which waited for: 3 -> 3; matrix products, arithmetic and copies ran while one was open for 0% -> 0% of each run, Pallas kernels for 0% -> 1%
where the time goes in v2:
time: 68.3 us; the launch traced here: 68 us
  blocking collectives  32.3 us (47%)
  waiting for transfers between devices  13.8 us (20%)
  starting transfers between devices  11.8 us (17%)
  Pallas kernels  7.72 us (11%)
  between operations  1.56 us (2%)
  local copies, waits for them, and re-layouts  0.73 us (1%)
    all_to_all x1, blocking collectives, on_device(): lax.all_to_all(hess.reshape(events, CELLS // events, Z), 'event', 0, 0, t...  18.9 us
    all_to_all x1, blocking collectives, on_device(): hess = lax.all_to_all(spread, 'event', 0, 0, tiled=True)  13.5 us
    ppermute x1, starting transfers between devices, on_device(): left = lax.ppermute(high, 'gy', [(i, i + 1) for i in range(count_y - 1)])  5.49 us
    ppermute x1, waiting for transfers between devices, on_device(): right = lax.ppermute(low, 'gy', [(i + 1, i) for i in range(count_y - 1)])  5.22 us
    ppermute x1, waiting for transfers between devices, on_device(): xb = lax.ppermute(xb, 'gx', swap(1))  5.12 us
    pallas_call x1, Pallas kernels, on_device(): pl.pallas_call(functools.partial(step_kernel, count_x, count_y), out_shap...  4.05 us
    ppermute x1, waiting for transfers between devices, on_device(): left = lax.ppermute(high, 'gy', [(i, i + 1) for i in range(count_y - 1)])  3.5 us
    pallas_call x1, Pallas kernels, on_device(): pl.pallas_call(begin_kernel, out_shape=(shape(Y_PLANES, X, Z), shape(Y_PL...  2.79 us
  transfers between devices with their start and end apart: 4, of which 3 were waited for; matrix products, arithmetic and copies ran while one was open for 0% of the time, Pallas kernels for 1%

profile of v2, /device:TPU:200, one launch (start us, length us, event | category | flops | bytes accessed | tf_op | source)
XLA Modules:
  0.0 68.0 jit_solution(7794652740102323146)
XLA Ops:
  0.6 0.0 copy-start
  0.6 0.0 copy-start.1
  0.7 0.0 copy-start.2
  0.7 0.0 copy-start.3
  0.7 0.0 copy-start.4
  0.7 0.0 copy-start.5
  0.7 0.0 copy-start.6
  0.7 0.0 copy-start.7
  0.7 0.0 copy-start.8
  0.7 0.0 copy-start.9
  0.7 0.0 copy-start.10
  0.7 2.8 %begin.1 = (f32[35,16,128]{2,1,0:T(8,128)}, f32[35,16,128]{2,1,0:T(8,128)}) custom-call(f32[3,256,128]{2,1,0:T(8,128)} %bitcast.28, f32[3,256,128]{2,1,0:T(8,128)} %bitcast.19, f32[3,256,128]{2,1,0:T(8,128)} %bitcast.30, f32[3,256,128]{2,1,0:T(8,128)} %bitcast.22, f32[3,256,128]{2,1,0:T(8,128)} %bitcast.25, f32[3,256,128]{2,1,0:T(8,128)} %bitcast.32, ...), custom_call_target="tpu_custom_call" | custom-call | tf_op jit(solution)/shard_map/begin/pallas_call | solution.py:421
  3.5 5.5 %collective-permute-start = (f32[35,16,128]{2,1,0:T(8,128)}, f32[35,16,128]{2,1,0:T(8,128)S(1)}, u32[]{:S(2)}, u32[]{:S(2)}) collective-permute-start(f32[35,16,128]{2,1,0:T(8,128)} %get-tuple-element.16), channel_id=1, source_target_pairs={{0,1},{1,2},{2,3},{3,4},{4,5},{5,6},{6,7},{7,8},{8,9},{9,10},{10,1... | collective-permute-start | bytes 860168 | tf_op jit(solution)/shard_map/ppermute | solution.py:432
  9.0 1.9 %collective-permute-start.1 = (f32[35,16,128]{2,1,0:T(8,128)}, f32[35,16,128]{2,1,0:T(8,128)S(1)}, u32[]{:S(2)}, u32[]{:S(2)}) collective-permute-start(f32[35,16,128]{2,1,0:T(8,128)} %get-tuple-element.17), channel_id=1, source_target_pairs={{1,0},{2,1},{3,2},{4,3},{5,4},{6,5},{7,6},{8,7},{9,8},{10,9},{11,1... | collective-permute-start | bytes 860168 | tf_op jit(solution)/shard_map/ppermute | solution.py:433
  11.0 0.0 copy-done
  11.0 0.0 copy-done.1
  11.0 0.0 copy-done.2
  11.0 0.0 copy-done.3
  11.0 0.0 copy-done.4
  11.0 0.0 copy-done.5
  11.0 0.0 copy-done.6
  11.0 0.0 copy-done.7
  11.0 0.0 copy-done.8
  11.1 0.0 copy-done.9
  11.1 0.0 copy-done.10
  11.1 0.8 %base.1 = (f32[9,256,128]{2,1,0:T(8,128)S(1)}, f32[616,128]{1,0:T(8,128)S(1)}, f32[616,128]{1,0:T(8,128)S(1)}) custom-call(f32[3,256,128]{2,1,0:T(8,128)S(1)} %bitcast.29, f32[3,256,128]{2,1,0:T(8,128)S(1)} %bitcast.20, f32[3,256,128]{2,1,0:T(8,128)S(1)} %bitcast.31, f32[3,256,128]{2,1,0:T(8,128)S(1)} %bitcast.23, f32[3,256,128]{2,1,0:T(8,128)S(1)} %bitcast.26, ...), custom_call_target="tpu_custom_call" | custom-call | tf_op jit(solution)/shard_map/base/pallas_call | solution.py:435
  11.9 0.0 copy-start.11
  11.9 0.0 copy-start.12
  11.9 0.0 copy-start.13
  11.9 3.5 %collective-permute-done.left_ref = f32[35,16,128]{2,1,0:T(8,128)S(1)} collective-permute-done((f32[35,16,128]{2,1,0:T(8,128)}, f32[35,16,128]{2,1,0:T(8,128)S(1)}, u32[]{:S(2)}, u32[]{:S(2)}) %collective-permute-start) | collective-permute-done | bytes 286752 | tf_op jit(solution)/shard_map/ppermute | solution.py:432
  15.4 5.2 %collective-permute-done.1.right_ref = f32[35,16,128]{2,1,0:T(8,128)S(1)} collective-permute-done((f32[35,16,128]{2,1,0:T(8,128)}, f32[35,16,128]{2,1,0:T(8,128)S(1)}, u32[]{:S(2)}, u32[]{:S(2)}) %collective-permute-start.1) | collective-permute-done | bytes 286752 | tf_op jit(solution)/shard_map/ppermute | solution.py:433
  20.6 0.1 widen.1
  20.7 1.9 %collective-permute-start.2 = (f32[616,128]{1,0:T(8,128)S(1)}, f32[616,128]{1,0:T(8,128)S(1)}, u32[]{:S(2)}, u32[]{:S(2)}) collective-permute-start(f32[616,128]{1,0:T(8,128)S(1)} %get-tuple-element.20), channel_id=1, source_target_pairs={{0,12},{12,0},{24,36},{36,24},{1,13},{13,1},{25,37},{37,25},{2,14}... | collective-permute-start | bytes 946184 | tf_op jit(solution)/shard_map/ppermute | solution.py:459
  22.7 2.5 %collective-permute-start.3 = (f32[616,128]{1,0:T(8,128)S(1)}, f32[616,128]{1,0:T(8,128)S(1)}, u32[]{:S(2)}, u32[]{:S(2)}) collective-permute-start(f32[616,128]{1,0:T(8,128)S(1)} %get-tuple-element.21), channel_id=1, source_target_pairs={{12,24},{24,12},{13,25},{25,13},{14,26},{26,14},{15,27},{27,15},{1... | collective-permute-start | bytes 946184 | tf_op jit(solution)/shard_map/ppermute | solution.py:460
  25.8 0.0 collective-permute-done.2.xa_ref
  25.8 5.1 %collective-permute-done.3.xb_ref = f32[616,128]{1,0:T(8,128)S(1)} collective-permute-done((f32[616,128]{1,0:T(8,128)S(1)}, f32[616,128]{1,0:T(8,128)S(1)}, u32[]{:S(2)}, u32[]{:S(2)}) %collective-permute-start.3) | collective-permute-done | bytes 315424 | tf_op jit(solution)/shard_map/ppermute | solution.py:460
  30.9 0.0 copy-done.11
  30.9 0.0 copy-done.12
  30.9 0.0 copy-done.13
  30.9 4.0 %step.1 = (f32[256,128]{1,0:T(8,128)S(1)}, f32[3,256,128]{2,1,0:T(8,128)}, f32[3,256,128]{2,1,0:T(8,128)}, f32[3,256,128]{2,1,0:T(8,128)}) custom-call(f32[3,256,128]{2,1,0:T(8,128)S(1)} %bitcast.21, f32[3,256,128]{2,1,0:T(8,128)S(1)} %bitcast.24, f32[3,256,128]{2,1,0:T(8,128)S(1)} %bitcast.27, f32[256,128]{1,0:T(8,128)S(1)} %bitcast.36, ...), custom_call_target="tpu_custom_call" | custom-call | tf_op jit(solution)/shard_map/step/pallas_call | solution.py:462
  35.0 18.9 %all_to_all.10 = f32[16,16,128]{2,1,0:T(8,128)S(1)} all-to-all(f32[16,16,128]{2,1,0:T(8,128)S(1)} %bitcast.39), channel_id=1, replica_groups=mesh['event'=16,'gx'=4,'gy'=12] {'event'}, dimensions={0} | all-to-all | bytes 262144 | tf_op jit(solution)/shard_map/all_to_all | solution.py:492
  53.9 13.5 %all_to_all.11 = f32[16,16,128]{2,1,0:T(8,128)S(1)} all-to-all(f32[16,16,128]{2,1,0:T(8,128)S(1)} %broadcast_in_dim.2), channel_id=1, replica_groups=mesh['event'=16,'gx'=4,'gy'=12] {'event'}, dimensions={0} | all-to-all | bytes 262144 | tf_op jit(solution)/shard_map/all_to_all | solution.py:495
  67.3 0.7 copy.21
  (3 shorter events, 0.0 us)
Async XLA Ops:
  0.6 10.3 %copy-start = (f32[1,3,16,16,128]{4,3,2,1,0:T(8,128)S(1)}, f32[1,3,16,16,128]{4,3,2,1,0:T(8,128)}, u32[]{:S(2)}) copy-start(f32[1,3,16,16,128]{4,3,2,1,0:T(8,128)} %param.16) | copy-start | bytes 1179652
  0.6 10.3 %copy-start.1 = (f32[1,3,16,16,128]{4,3,2,1,0:T(8,128)S(1)}, f32[1,3,16,16,128]{4,3,2,1,0:T(8,128)}, u32[]{:S(2)}) copy-start(f32[1,3,16,16,128]{4,3,2,1,0:T(8,128)} %param.18) | copy-start | bytes 1179652
  0.7 10.3 %copy-start.2 = (f32[1,3,16,16,128]{4,3,2,1,0:T(8,128)S(1)}, f32[1,3,16,16,128]{4,3,2,1,0:T(8,128)}, u32[]{:S(2)}) copy-start(f32[1,3,16,16,128]{4,3,2,1,0:T(8,128)} %param.19) | copy-start | bytes 1179652
  0.7 10.3 %copy-start.3 = (f32[1,3,16,16,128]{4,3,2,1,0:T(8,128)S(1)}, f32[1,3,16,16,128]{4,3,2,1,0:T(8,128)}, u32[]{:S(2)}) copy-start(f32[1,3,16,16,128]{4,3,2,1,0:T(8,128)} %param.15) | copy-start | bytes 1179652
  0.7 10.3 %copy-start.4 = (f32[1,3,16,16,128]{4,3,2,1,0:T(8,128)S(1)}, f32[1,3,16,16,128]{4,3,2,1,0:T(8,128)}, u32[]{:S(2)}) copy-start(f32[1,3,16,16,128]{4,3,2,1,0:T(8,128)} %param.17) | copy-start | bytes 1179652
  0.7 10.3 %copy-start.5 = (f32[1,3,16,16,128]{4,3,2,1,0:T(8,128)S(1)}, f32[1,3,16,16,128]{4,3,2,1,0:T(8,128)}, u32[]{:S(2)}) copy-start(f32[1,3,16,16,128]{4,3,2,1,0:T(8,128)} %param.20) | copy-start | bytes 1179652
  0.7 10.3 %copy-start.6 = (f32[16,16,128]{2,1,0:T(8,128)S(1)}, f32[16,16,128]{2,1,0:T(8,128)}, u32[]{:S(2)}) copy-start(f32[16,16,128]{2,1,0:T(8,128)} %param.21) | copy-start | bytes 393220
  0.7 10.3 %copy-start.7 = (f32[3,3,1,1,1024]{4,3,2,1,0:T(1,128)S(1)}, f32[3,3,1,1,1024]{4,3,2,1,0:T(1,128)}, u32[]{:S(2)}) copy-start(f32[3,3,1,1,1024]{4,3,2,1,0:T(1,128)} %param.26) | copy-start | bytes 110596
  0.7 10.3 %copy-start.8 = (f32[1,3,1,1,1024]{4,3,2,1,0:T(1,128)S(1)}, f32[1,3,1,1,1024]{4,3,2,1,0:T(1,128)}, u32[]{:S(2)}) copy-start(f32[1,3,1,1,1024]{4,3,2,1,0:T(1,128)} %param.27) | copy-start | bytes 36868
  0.7 10.3 %copy-start.9 = (s32[1,1,1024]{2,1,0:T(1,128)S(1)}, s32[1,1,1024]{2,1,0:T(1,128)}, u32[]{:S(2)}) copy-start(s32[1,1,1024]{2,1,0:T(1,128)} %param.25) | copy-start | bytes 12292
  0.7 10.3 %copy-start.10 = (f32[128]{0:T(128)S(1)}, f32[128]{0:T(128)}, u32[]{:S(2)}) copy-start(f32[128]{0:T(128)} %param.24) | copy-start | bytes 1540
  3.5 11.9 %collective-permute-start = (f32[35,16,128]{2,1,0:T(8,128)}, f32[35,16,128]{2,1,0:T(8,128)S(1)}, u32[]{:S(2)}, u32[]{:S(2)}) collective-permute-start(f32[35,16,128]{2,1,0:T(8,128)} %get-tuple-element.16), channel_id=1, source_target_pairs={{0,1},{1,2},{2,3},{3,4},{4,5},{5,6},{6,7},{7,8},{8,9},{9,10},{10,1... | collective-permute-start | bytes 860168 | tf_op jit(solution)/shard_map/ppermute | solution.py:432
  9.0 11.6 %collective-permute-start.1 = (f32[35,16,128]{2,1,0:T(8,128)}, f32[35,16,128]{2,1,0:T(8,128)S(1)}, u32[]{:S(2)}, u32[]{:S(2)}) collective-permute-start(f32[35,16,128]{2,1,0:T(8,128)} %get-tuple-element.17), channel_id=1, source_target_pairs={{1,0},{2,1},{3,2},{4,3},{5,4},{6,5},{7,6},{8,7},{9,8},{10,9},{11,1... | collective-permute-start | bytes 860168 | tf_op jit(solution)/shard_map/ppermute | solution.py:433
  11.9 19.0 %copy-start.11 = (f32[128]{0:T(128)S(1)}, f32[128]{0:T(128)}, u32[]{:S(2)}) copy-start(f32[128]{0:T(128)} %param.22) | copy-start | bytes 1540
  11.9 19.0 %copy-start.12 = (f32[128]{0:T(128)S(1)}, f32[128]{0:T(128)}, u32[]{:S(2)}) copy-start(f32[128]{0:T(128)} %param.23) | copy-start | bytes 1540
  11.9 19.0 %copy-start.13 = (f32[1,3]{1,0:T(1,128)S(1)}, f32[1,3]{1,0:T(1,128)}, u32[]{:S(2)}) copy-start(f32[1,3]{1,0:T(1,128)} %force_ref.1) | copy-start | bytes 40
  20.7 5.1 %collective-permute-start.2 = (f32[616,128]{1,0:T(8,128)S(1)}, f32[616,128]{1,0:T(8,128)S(1)}, u32[]{:S(2)}, u32[]{:S(2)}) collective-permute-start(f32[616,128]{1,0:T(8,128)S(1)} %get-tuple-element.20), channel_id=1, source_target_pairs={{0,12},{12,0},{24,36},{36,24},{1,13},{13,1},{25,37},{37,25},{2,14}... | collective-permute-start | bytes 946184 | tf_op jit(solution)/shard_map/ppermute | solution.py:459
  22.7 8.3 %collective-permute-start.3 = (f32[616,128]{1,0:T(8,128)S(1)}, f32[616,128]{1,0:T(8,128)S(1)}, u32[]{:S(2)}, u32[]{:S(2)}) collective-permute-start(f32[616,128]{1,0:T(8,128)S(1)} %get-tuple-element.21), channel_id=1, source_target_pairs={{12,24},{24,12},{13,25},{25,13},{14,26},{26,14},{15,27},{27,15},{1... | collective-permute-start | bytes 946184 | tf_op jit(solution)/shard_map/ppermute | solution.py:460

commit v3 on v2

--- a/solution.py
+++ b/solution.py
@@ -14,11 +14,11 @@
 LAYER = 4
 ELEMS = CELLS * LAYER
 
-Y_BASE = 27
-Y_PERT = 33
-Y_PLANES = 35
-
-X_STEP = 54
+Y_BASE = 18
+Y_PERT = 24
+Y_PLANES = 26
+
+X_STEP = 38
 X_PERT = 9 * X_STEP
 X_BASE = X_PERT + 34
 X_ROWS = X_BASE + 6 * Y
@@ -30,7 +30,7 @@
 
 
 def now_row(c, d):
-    return c * X_STEP + (0, 20, 38)[d - 1]
+    return c * X_STEP + (0, 20)[d - 1]
 
 
 def pert_row(d):
@@ -75,22 +75,43 @@
     return applied
 
 
+def edge_coefficients(shear, lame, along):
+    return [2.0 * shear + lame if i == along else shear for i in range(3)]
+
+
+def edge_bases(lame_ref, shear_ref, buoy_ref, along, bases, far, pert):
+    scale = 0.1 * buoy_ref[...].reshape(1, Z)
+    top = lax.broadcasted_iota(jnp.int32, (1, Z), 1) == 0
+    surface_scale = jnp.where(top, scale, 0.0)
+    quarter = 0.25 * scale
+    coefficients = edge_coefficients(
+        quarter * shear_ref[...].reshape(1, Z), quarter * lame_ref[...].reshape(1, Z), along
+    )
+    forward, adjoint = [], []
+    for i in range(3):
+        moved = quarter * pert * (2.0 if i == along else 1.0)
+        forward.append(bases[0][i] + coefficients[i] * far[0][i])
+        born = bases[1][i] + coefficients[i] * far[1][i] + moved * far[0][i]
+        adjoint.append(bases[2][i] + coefficients[i] * far[2][i] + surface_scale * born)
+    return forward + adjoint
+
+
 def plane_rows(ref, y):
     return ref[pl.ds(y, X, stride=Y), :]
 
 
 def begin_kernel(*refs):
-    sources, low_ref, high_ref = refs[:11], refs[11], refs[12]
-    held, arrived = refs[13:24], refs[24]
+    sources, low_ref, high_ref = refs[:13], refs[13], refs[14]
+    held, arrived = refs[15:28], refs[28]
     copies = [
         pltpu.make_async_copy(source, ref, arrived.at[i])
         for i, (source, ref) in enumerate(zip(sources, held))
     ]
-    order = (8, 9, 10, 1, 3, 4, 6, 7, 0, 2, 5)
+    order = (8, 9, 10, 1, 3, 4, 6, 7, 11, 12, 0, 2, 5)
     for i in order:
         copies[i].start()
     fprev_ref, fnow_ref, bprev_ref, bnow_ref, anow_ref, anext_ref = held[:6]
-    pert_ref, buoy_ref, cells_ref, matrix_ref, motion_ref = held[6:]
+    pert_ref, buoy_ref, cells_ref, matrix_ref, motion_ref, lame_ref, shear_ref = held[6:]
     for i in order[:3]:
         copies[i].wait()
 
@@ -98,35 +119,33 @@
     columns = (row % X) * Y + jnp.where(row < X, 0, Y - 1)
     applied = placed_force(columns, cells_ref, matrix_ref, motion_ref)
 
-    for i in order[3:7]:
+    for i in order[3:9]:
         copies[i].wait()
     now = [r.at[i] for r in (fnow_ref, bnow_ref, anow_ref) for i in range(3)]
     for c in range(9):
-        for k in range(3):
-            low_ref[3 * c + k] = plane_rows(now[c], k)
-            high_ref[3 * c + k] = plane_rows(now[c], Y - 3 + k)
+        for k in range(2):
+            low_ref[2 * c + k] = plane_rows(now[c], k)
+            high_ref[2 * c + k] = plane_rows(now[c], Y - 2 + k)
     for k in range(2):
         low_ref[Y_PERT + k] = plane_rows(pert_ref, k)
         high_ref[Y_PERT + k] = plane_rows(pert_ref, Y - 2 + k)
 
-    for i in order[7:]:
+    for i in order[9:]:
         copies[i].wait()
     scale = 0.1 * buoy_ref[...].reshape(1, Z)
-    top = lax.broadcasted_iota(jnp.int32, (1, Z), 1) == 0
-    surface_scale = jnp.where(top, scale, 0.0)
-    for ref, y, first in ((low_ref, 0, 0), (high_ref, Y - 1, X)):
+    for ref, y, step, first in ((low_ref, 0, 1, 0), (high_ref, Y - 1, -1, X)):
+        bases = [
+            [2.0 * plane_rows(now[3 * f + i], y) - plane_rows(old.at[i], y) for i in range(3)]
+            for f, old in enumerate((fprev_ref, bprev_ref, anext_ref))
+        ]
         for i in range(3):
-            ref[Y_BASE + i] = (
-                2.0 * plane_rows(now[i], y)
-                - plane_rows(fprev_ref.at[i], y)
-                + scale * applied[i][first : first + X]
-            )
-            born = 2.0 * plane_rows(now[3 + i], y) - plane_rows(bprev_ref.at[i], y)
-            ref[Y_BASE + 3 + i] = (
-                2.0 * plane_rows(now[6 + i], y)
-                - plane_rows(anext_ref.at[i], y)
-                + surface_scale * born
-            )
+            bases[0][i] = bases[0][i] + scale * applied[i][first : first + X]
+        far = [[plane_rows(now[3 * f + i], y + 2 * step) for i in range(3)] for f in range(3)]
+        sent = edge_bases(
+            lame_ref, shear_ref, buoy_ref, 1, bases, far, plane_rows(pert_ref, y + step)
+        )
+        for c in range(6):
+            ref[Y_BASE + c] = sent[c]
 
 
 def base_kernel(
@@ -141,6 +160,8 @@
     cells_ref,
     matrix_ref,
     motion_ref,
+    lame_ref,
+    shear_ref,
     base_ref,
     xa_ref,
     xb_ref,
@@ -157,7 +178,6 @@
         base_ref[6 + i] = 2.0 * anow_ref[i] - anext_ref[i] + surface_scale * born
 
     now = [r.at[i] for r in (fnow_ref, bnow_ref, anow_ref) for i in range(3)]
-    bases = [base_ref.at[i] for i in (0, 1, 2, 6, 7, 8)]
     odd = lax.axis_index("gx") % 2 == 1
     for ref, high in ((xa_ref, jnp.logical_not(odd)), (xb_ref, odd)):
 
@@ -166,12 +186,19 @@
             return source[pl.ds(start, Y), :]
 
         for c in range(9):
-            for d in (1, 2, 3):
+            for d in (1, 2):
                 ref[pl.ds(now_row(c, d) + 3 - d, Y), :] = plane_of(now[c], d)
         for d in (1, 2):
             ref[pl.ds(pert_row(d) + 2 - d, Y), :] = plane_of(pert_ref, d)
+        bases = [[plane_of(base_ref.at[3 * f + i], 1) for i in range(3)] for f in range(3)]
+        for i in range(3):
+            bases[2][i] = 2.0 * plane_of(now[6 + i], 1) - plane_of(anext_ref.at[i], 1)
+        far = [[plane_of(now[3 * f + i], 3) for i in range(3)] for f in range(3)]
+        sent = edge_bases(
+            lame_ref, shear_ref, buoy_ref, 0, bases, far, plane_of(pert_ref, 2)
+        )
         for c in range(6):
-            ref[pl.ds(X_BASE + c * Y, Y), :] = plane_of(bases[c], 1)
+            ref[pl.ds(X_BASE + c * Y, Y), :] = sent[c]
 
 
 def widen_kernel(xa_in, xb_in, left_ref, right_ref, xa_ref, xb_ref):
@@ -183,8 +210,8 @@
             for c in range(9):
                 start = now_row(c, d)
                 for k in range(3 - d):
-                    ref[pl.ds(start + k, 1), :] = left_ref[3 * c + d + k, pl.ds(x, 1), :]
-                    ref[pl.ds(start + 19 - d + k, 1), :] = right_ref[3 * c + k, pl.ds(x, 1), :]
+                    ref[pl.ds(start + k, 1), :] = left_ref[2 * c + d - 1 + k, pl.ds(x, 1), :]
+                    ref[pl.ds(start + 19 - d + k, 1), :] = right_ref[2 * c + k, pl.ds(x, 1), :]
         x = near_x(high, 1)
         ref[pl.ds(pert_row(1), 1), :] = left_ref[Y_PERT + 1, pl.ds(x, 1), :]
         ref[pl.ds(pert_row(1) + 17, 1), :] = right_ref[Y_PERT, pl.ds(x, 1), :]
@@ -223,9 +250,13 @@
     for c in range(9):
         for x in range(X):
             wide[c, pl.ds((x + 3) * ROWS + ZERO, Y), :] = now[c][pl.ds(x * Y, Y), :]
-        for k in range(3):
-            wide[c, pl.ds(3 * ROWS + ZERO - 3 + k, X, stride=ROWS), :] = left_ref[3 * c + k]
-            wide[c, pl.ds(3 * ROWS + ZERO + Y + k, X, stride=ROWS), :] = right_ref[3 * c + k]
+        for k in range(2):
+            wide[c, pl.ds(3 * ROWS + ZERO - 2 + k, X, stride=ROWS), :] = left_ref[2 * c + k]
+            wide[c, pl.ds(3 * ROWS + ZERO + Y + k, X, stride=ROWS), :] = right_ref[2 * c + k]
+        for row in (ZERO - 3, ZERO + Y + 2):
+            wide[c, pl.ds(3 * ROWS + row, X, stride=ROWS), :] = jnp.zeros((X, Z), F32)
+        for plane in (0, X + 5):
+            wide[c, pl.ds(plane * ROWS + ZERO, Y), :] = jnp.zeros((Y, Z), F32)
     for x in range(X):
         pert[pl.ds((x + 2) * ROWS + ZERO, Y), :] = pert_in[pl.ds(x * Y, Y), :]
     for k in range(2):
@@ -238,17 +269,16 @@
         new[c, pl.ds(ROWS + ZERO + Y, X, stride=ROWS), :] = right_ref[Y_BASE + c]
     odd = index_x % 2 == 1
     for ref, high in ((xa_ref, jnp.logical_not(odd)), (xb_ref, odd)):
-        for d in (1, 2, 3):
+        for d in (1, 2):
             x = jnp.where(high, X - 1 + d, -d)
             rows = Y + 2 * (3 - d)
             for c in range(9):
                 wide[c, pl.ds((x + 3) * ROWS + ZERO - (3 - d), rows), :] = ref[
                     pl.ds(now_row(c, d), rows), :
                 ]
-            if d < 3:
-                pert[pl.ds((x + 2) * ROWS + ZERO - (2 - d), rows - 2), :] = ref[
-                    pl.ds(pert_row(d), rows - 2), :
-                ]
+            pert[pl.ds((x + 2) * ROWS + ZERO - (2 - d), rows - 2), :] = ref[
+                pl.ds(pert_row(d), rows - 2), :
+            ]
             if d == 1:
                 for c in range(6):
                     new[c, pl.ds((x + 1) * ROWS + ZERO, Y), :] = ref[pl.ds(X_BASE + c * Y, Y), :]
@@ -417,14 +447,16 @@
         drm_cells.reshape(1, ELEMS),
         drm_matrix.reshape(9, 1, ELEMS),
         drm_motion.reshape(3, 1, ELEMS),
+        lame,
+        shear,
     )
     low, high = pl.pallas_call(
         begin_kernel,
         out_shape=(shape(Y_PLANES, X, Z), shape(Y_PLANES, X, Z)),
-        in_specs=[HBM] * 11,
+        in_specs=[HBM] * 13,
         out_specs=[VMEM] * 2,
         scratch_shapes=[pltpu.VMEM(a.shape, a.dtype) for a in begin_inputs]
-        + [pltpu.SemaphoreType.DMA((11,))],
+        + [pltpu.SemaphoreType.DMA((13,))],
         compiler_params=pltpu.CompilerParams(vmem_limit_bytes=60 * 2**20),
         name="begin",
     )(*begin_inputs)
@@ -435,7 +467,7 @@
     base, xa, xb = pl.pallas_call(
         base_kernel,
         out_shape=(shape(9, CELLS, Z), shape(X_ROWS, Z), shape(X_ROWS, Z)),
-        in_specs=[VMEM] * 11,
+        in_specs=[VMEM] * 13,
         out_specs=[VMEM] * 3,
         compiler_params=pltpu.CompilerParams(vmem_limit_bytes=16 * 2**20),
         name="base",

time: 68.3 us -> 66 us (0.966)
  waiting for transfers between devices: 13.8 us -> 11.5 us
    ppermute x1, waiting for transfers between devices: 3.5 us -> 1.93 us  [on_device(): left = lax.ppermute(high, 'gy', [(i, i + 1) for i in range(count_y - 1)])]
    ppermute x1, waiting for transfers between devices: 5.12 us -> 4.33 us  [on_device(): xb = lax.ppermute(xb, 'gx', swap(1))]
where the time goes in v3:
time: 66 us; the launch traced here: 65.7 us
  blocking collectives  32.3 us (49%)
  starting transfers between devices  11.8 us (18%)
  waiting for transfers between devices  11.5 us (17%)
  Pallas kernels  7.72 us (12%)
  between operations  1.58 us (2%)
  local copies, waits for them, and re-layouts  0.73 us (1%)
    all_to_all x1, blocking collectives, on_device(): lax.all_to_all(hess.reshape(events, CELLS // events, Z), 'event', 0, 0, t...  18.9 us
    all_to_all x1, blocking collectives, on_device(): hess = lax.all_to_all(spread, 'event', 0, 0, tiled=True)  13.5 us
    ppermute x1, starting transfers between devices, on_device(): left = lax.ppermute(high, 'gy', [(i, i + 1) for i in range(count_y - 1)])  5.49 us
    ppermute x1, waiting for transfers between devices, on_device(): right = lax.ppermute(low, 'gy', [(i + 1, i) for i in range(count_y - 1)])  5.23 us
    ppermute x1, waiting for transfers between devices, on_device(): xb = lax.ppermute(xb, 'gx', swap(1))  4.33 us
    pallas_call x1, Pallas kernels, on_device(): pl.pallas_call(functools.partial(step_kernel, count_x, count_y), out_shap...  4.1 us
    pallas_call x1, Pallas kernels, on_device(): pl.pallas_call(begin_kernel, out_shape=(shape(Y_PLANES, X, Z), shape(Y_PL...  2.75 us
    ppermute x1, starting transfers between devices, on_device(): xb = lax.ppermute(xb, 'gx', swap(1))  2.46 us
  transfers between devices with their start and end apart: 4, of which 3 were waited for; matrix products, arithmetic and copies ran while one was open for 0% of the time, Pallas kernels for 1%

profile of v3, /device:TPU:200, one launch (start us, length us, event | category | flops | bytes accessed | tf_op | source)
XLA Modules:
  0.0 65.7 jit_solution(1292078092660123742)
XLA Ops:
  0.6 0.0 copy-start
  0.6 0.0 copy-start.1
  0.7 0.0 copy-start.2
  0.7 0.0 copy-start.3
  0.7 0.0 copy-start.4
  0.7 0.0 copy-start.5
  0.7 0.0 copy-start.6
  0.7 0.0 copy-start.7
  0.7 0.0 copy-start.8
  0.7 0.0 copy-start.9
  0.7 0.0 copy-start.10
  0.7 0.0 copy-start.11
  0.8 0.0 copy-start.12
  0.8 2.8 %begin.1 = (f32[26,16,128]{2,1,0:T(8,128)}, f32[26,16,128]{2,1,0:T(8,128)}) custom-call(f32[3,256,128]{2,1,0:T(8,128)} %bitcast.28, f32[3,256,128]{2,1,0:T(8,128)} %bitcast.19, f32[3,256,128]{2,1,0:T(8,128)} %bitcast.30, f32[3,256,128]{2,1,0:T(8,128)} %bitcast.22, f32[3,256,128]{2,1,0:T(8,128)} %bitcast.25, f32[3,256,128]{2,1,0:T(8,128)} %bitcast.32, ...), custom_call_target="tpu_custom_call" | custom-call | tf_op jit(solution)/shard_map/begin/pallas_call | solution.py:453
  3.5 5.5 %collective-permute-start = (f32[26,16,128]{2,1,0:T(8,128)}, f32[26,16,128]{2,1,0:T(8,128)S(1)}, u32[]{:S(2)}, u32[]{:S(2)}) collective-permute-start(f32[26,16,128]{2,1,0:T(8,128)} %get-tuple-element.16), channel_id=1, source_target_pairs={{0,1},{1,2},{2,3},{3,4},{4,5},{5,6},{6,7},{7,8},{8,9},{9,10},{10,1... | collective-permute-start | bytes 638984 | tf_op jit(solution)/shard_map/ppermute | solution.py:464
  9.0 0.0 copy-start.13
  9.0 1.9 %collective-permute-start.1 = (f32[26,16,128]{2,1,0:T(8,128)}, f32[26,16,128]{2,1,0:T(8,128)S(1)}, u32[]{:S(2)}, u32[]{:S(2)}) collective-permute-start(f32[26,16,128]{2,1,0:T(8,128)} %get-tuple-element.17), channel_id=1, source_target_pairs={{1,0},{2,1},{3,2},{4,3},{5,4},{6,5},{7,6},{8,7},{9,8},{10,9},{11,1... | collective-permute-start | bytes 638984 | tf_op jit(solution)/shard_map/ppermute | solution.py:465
  11.0 0.0 copy-done
  11.0 0.0 copy-done.1
  11.0 0.0 copy-done.2
  11.0 0.0 copy-done.3
  11.0 0.0 copy-done.4
  11.0 0.0 copy-done.5
  11.0 0.0 copy-done.6
  11.0 0.0 copy-done.7
  11.0 0.0 copy-done.8
  11.1 0.0 copy-done.9
  11.1 0.0 copy-done.10
  11.1 0.0 copy-done.11
  11.1 0.0 copy-done.12
  11.1 0.8 %base.1 = (f32[9,256,128]{2,1,0:T(8,128)S(1)}, f32[472,128]{1,0:T(8,128)S(1)}, f32[472,128]{1,0:T(8,128)S(1)}) custom-call(f32[3,256,128]{2,1,0:T(8,128)S(1)} %bitcast.29, f32[3,256,128]{2,1,0:T(8,128)S(1)} %bitcast.20, f32[3,256,128]{2,1,0:T(8,128)S(1)} %bitcast.31, f32[3,256,128]{2,1,0:T(8,128)S(1)} %bitcast.23, f32[3,256,128]{2,1,0:T(8,128)S(1)} %bitcast.26, ...), custom_call_target="tpu_custom_call" | custom-call | tf_op jit(solution)/shard_map/base/pallas_call | solution.py:467
  11.9 1.9 %collective-permute-done.left_ref = f32[26,16,128]{2,1,0:T(8,128)S(1)} collective-permute-done((f32[26,16,128]{2,1,0:T(8,128)}, f32[26,16,128]{2,1,0:T(8,128)S(1)}, u32[]{:S(2)}, u32[]{:S(2)}) %collective-permute-start) | collective-permute-done | bytes 213024 | tf_op jit(solution)/shard_map/ppermute | solution.py:464
  13.8 5.2 %collective-permute-done.1.right_ref = f32[26,16,128]{2,1,0:T(8,128)S(1)} collective-permute-done((f32[26,16,128]{2,1,0:T(8,128)}, f32[26,16,128]{2,1,0:T(8,128)S(1)}, u32[]{:S(2)}, u32[]{:S(2)}) %collective-permute-start.1) | collective-permute-done | bytes 213024 | tf_op jit(solution)/shard_map/ppermute | solution.py:465
  19.1 0.1 widen.1
  19.1 1.9 %collective-permute-start.2 = (f32[472,128]{1,0:T(8,128)S(1)}, f32[472,128]{1,0:T(8,128)S(1)}, u32[]{:S(2)}, u32[]{:S(2)}) collective-permute-start(f32[472,128]{1,0:T(8,128)S(1)} %get-tuple-element.20), channel_id=1, source_target_pairs={{0,12},{12,0},{24,36},{36,24},{1,13},{13,1},{25,37},{37,25},{2,14}... | collective-permute-start | bytes 725000 | tf_op jit(solution)/shard_map/ppermute | solution.py:491
  21.1 2.5 %collective-permute-start.3 = (f32[472,128]{1,0:T(8,128)S(1)}, f32[472,128]{1,0:T(8,128)S(1)}, u32[]{:S(2)}, u32[]{:S(2)}) collective-permute-start(f32[472,128]{1,0:T(8,128)S(1)} %get-tuple-element.21), channel_id=1, source_target_pairs={{12,24},{24,12},{13,25},{25,13},{14,26},{26,14},{15,27},{27,15},{1... | collective-permute-start | bytes 725000 | tf_op jit(solution)/shard_map/ppermute | solution.py:492
  24.2 0.0 collective-permute-done.2.xa_ref
  24.2 4.3 %collective-permute-done.3.xb_ref = f32[472,128]{1,0:T(8,128)S(1)} collective-permute-done((f32[472,128]{1,0:T(8,128)S(1)}, f32[472,128]{1,0:T(8,128)S(1)}, u32[]{:S(2)}, u32[]{:S(2)}) %collective-permute-start.3) | collective-permute-done | bytes 241696 | tf_op jit(solution)/shard_map/ppermute | solution.py:492
  28.5 0.0 copy-done.13
  28.5 4.1 %step.1 = (f32[256,128]{1,0:T(8,128)S(1)}, f32[3,256,128]{2,1,0:T(8,128)}, f32[3,256,128]{2,1,0:T(8,128)}, f32[3,256,128]{2,1,0:T(8,128)}) custom-call(f32[3,256,128]{2,1,0:T(8,128)S(1)} %bitcast.21, f32[3,256,128]{2,1,0:T(8,128)S(1)} %bitcast.24, f32[3,256,128]{2,1,0:T(8,128)S(1)} %bitcast.27, f32[256,128]{1,0:T(8,128)S(1)} %bitcast.36, ...), custom_call_target="tpu_custom_call" | custom-call | tf_op jit(solution)/shard_map/step/pallas_call | solution.py:494
  32.6 18.9 %all_to_all.10 = f32[16,16,128]{2,1,0:T(8,128)S(1)} all-to-all(f32[16,16,128]{2,1,0:T(8,128)S(1)} %bitcast.39), channel_id=1, replica_groups=mesh['event'=16,'gx'=4,'gy'=12] {'event'}, dimensions={0} | all-to-all | bytes 262144 | tf_op jit(solution)/shard_map/all_to_all | solution.py:524
  51.5 13.5 %all_to_all.11 = f32[16,16,128]{2,1,0:T(8,128)S(1)} all-to-all(f32[16,16,128]{2,1,0:T(8,128)S(1)} %broadcast_in_dim.2), channel_id=1, replica_groups=mesh['event'=16,'gx'=4,'gy'=12] {'event'}, dimensions={0} | all-to-all | bytes 262144 | tf_op jit(solution)/shard_map/all_to_all | solution.py:527
  65.0 0.7 copy.21
  (3 shorter events, 0.0 us)
Async XLA Ops:
  0.6 10.3 %copy-start = (f32[1,3,16,16,128]{4,3,2,1,0:T(8,128)S(1)}, f32[1,3,16,16,128]{4,3,2,1,0:T(8,128)}, u32[]{:S(2)}) copy-start(f32[1,3,16,16,128]{4,3,2,1,0:T(8,128)} %param.16) | copy-start | bytes 1179652
  0.6 10.3 %copy-start.1 = (f32[1,3,16,16,128]{4,3,2,1,0:T(8,128)S(1)}, f32[1,3,16,16,128]{4,3,2,1,0:T(8,128)}, u32[]{:S(2)}) copy-start(f32[1,3,16,16,128]{4,3,2,1,0:T(8,128)} %param.18) | copy-start | bytes 1179652
  0.7 10.3 %copy-start.2 = (f32[1,3,16,16,128]{4,3,2,1,0:T(8,128)S(1)}, f32[1,3,16,16,128]{4,3,2,1,0:T(8,128)}, u32[]{:S(2)}) copy-start(f32[1,3,16,16,128]{4,3,2,1,0:T(8,128)} %param.19) | copy-start | bytes 1179652
  0.7 10.3 %copy-start.3 = (f32[1,3,16,16,128]{4,3,2,1,0:T(8,128)S(1)}, f32[1,3,16,16,128]{4,3,2,1,0:T(8,128)}, u32[]{:S(2)}) copy-start(f32[1,3,16,16,128]{4,3,2,1,0:T(8,128)} %param.15) | copy-start | bytes 1179652
  0.7 10.3 %copy-start.4 = (f32[1,3,16,16,128]{4,3,2,1,0:T(8,128)S(1)}, f32[1,3,16,16,128]{4,3,2,1,0:T(8,128)}, u32[]{:S(2)}) copy-start(f32[1,3,16,16,128]{4,3,2,1,0:T(8,128)} %param.17) | copy-start | bytes 1179652
  0.7 10.3 %copy-start.5 = (f32[1,3,16,16,128]{4,3,2,1,0:T(8,128)S(1)}, f32[1,3,16,16,128]{4,3,2,1,0:T(8,128)}, u32[]{:S(2)}) copy-start(f32[1,3,16,16,128]{4,3,2,1,0:T(8,128)} %param.20) | copy-start | bytes 1179652
  0.7 10.3 %copy-start.6 = (f32[16,16,128]{2,1,0:T(8,128)S(1)}, f32[16,16,128]{2,1,0:T(8,128)}, u32[]{:S(2)}) copy-start(f32[16,16,128]{2,1,0:T(8,128)} %param.21) | copy-start | bytes 393220
  0.7 10.3 %copy-start.7 = (f32[3,3,1,1,1024]{4,3,2,1,0:T(1,128)S(1)}, f32[3,3,1,1,1024]{4,3,2,1,0:T(1,128)}, u32[]{:S(2)}) copy-start(f32[3,3,1,1,1024]{4,3,2,1,0:T(1,128)} %param.26) | copy-start | bytes 110596
  0.7 10.3 %copy-start.8 = (f32[1,3,1,1,1024]{4,3,2,1,0:T(1,128)S(1)}, f32[1,3,1,1,1024]{4,3,2,1,0:T(1,128)}, u32[]{:S(2)}) copy-start(f32[1,3,1,1,1024]{4,3,2,1,0:T(1,128)} %param.27) | copy-start | bytes 36868
  0.7 10.3 %copy-start.9 = (s32[1,1,1024]{2,1,0:T(1,128)S(1)}, s32[1,1,1024]{2,1,0:T(1,128)}, u32[]{:S(2)}) copy-start(s32[1,1,1024]{2,1,0:T(1,128)} %param.25) | copy-start | bytes 12292
  0.7 10.3 %copy-start.10 = (f32[128]{0:T(128)S(1)}, f32[128]{0:T(128)}, u32[]{:S(2)}) copy-start(f32[128]{0:T(128)} %param.24) | copy-start | bytes 1540
  0.7 10.3 %copy-start.11 = (f32[128]{0:T(128)S(1)}, f32[128]{0:T(128)}, u32[]{:S(2)}) copy-start(f32[128]{0:T(128)} %param.22) | copy-start | bytes 1540
  0.8 10.3 %copy-start.12 = (f32[128]{0:T(128)S(1)}, f32[128]{0:T(128)}, u32[]{:S(2)}) copy-start(f32[128]{0:T(128)} %param.23) | copy-start | bytes 1540
  3.5 10.3 %collective-permute-start = (f32[26,16,128]{2,1,0:T(8,128)}, f32[26,16,128]{2,1,0:T(8,128)S(1)}, u32[]{:S(2)}, u32[]{:S(2)}) collective-permute-start(f32[26,16,128]{2,1,0:T(8,128)} %get-tuple-element.16), channel_id=1, source_target_pairs={{0,1},{1,2},{2,3},{3,4},{4,5},{5,6},{6,7},{7,8},{8,9},{9,10},{10,1... | collective-permute-start | bytes 638984 | tf_op jit(solution)/shard_map/ppermute | solution.py:464
  9.0 19.5 %copy-start.13 = (f32[1,3]{1,0:T(1,128)S(1)}, f32[1,3]{1,0:T(1,128)}, u32[]{:S(2)}) copy-start(f32[1,3]{1,0:T(1,128)} %force_ref.1) | copy-start | bytes 40
  9.0 10.0 %collective-permute-start.1 = (f32[26,16,128]{2,1,0:T(8,128)}, f32[26,16,128]{2,1,0:T(8,128)S(1)}, u32[]{:S(2)}, u32[]{:S(2)}) collective-permute-start(f32[26,16,128]{2,1,0:T(8,128)} %get-tuple-element.17), channel_id=1, source_target_pairs={{1,0},{2,1},{3,2},{4,3},{5,4},{6,5},{7,6},{8,7},{9,8},{10,9},{11,1... | collective-permute-start | bytes 638984 | tf_op jit(solution)/shard_map/ppermute | solution.py:465
  19.1 5.1 %collective-permute-start.2 = (f32[472,128]{1,0:T(8,128)S(1)}, f32[472,128]{1,0:T(8,128)S(1)}, u32[]{:S(2)}, u32[]{:S(2)}) collective-permute-start(f32[472,128]{1,0:T(8,128)S(1)} %get-tuple-element.20), channel_id=1, source_target_pairs={{0,12},{12,0},{24,36},{36,24},{1,13},{13,1},{25,37},{37,25},{2,14}... | collective-permute-start | bytes 725000 | tf_op jit(solution)/shard_map/ppermute | solution.py:491
  21.1 7.5 %collective-permute-start.3 = (f32[472,128]{1,0:T(8,128)S(1)}, f32[472,128]{1,0:T(8,128)S(1)}, u32[]{:S(2)}, u32[]{:S(2)}) collective-permute-start(f32[472,128]{1,0:T(8,128)S(1)} %get-tuple-element.21), channel_id=1, source_target_pairs={{12,24},{24,12},{13,25},{25,13},{14,26},{26,14},{15,27},{27,15},{1... | collective-permute-start | bytes 725000 | tf_op jit(solution)/shard_map/ppermute | solution.py:492

commit v4 on v3

--- a/solution.py
+++ b/solution.py
@@ -201,7 +201,7 @@
             ref[pl.ds(X_BASE + c * Y, Y), :] = sent[c]
 
 
-def widen_kernel(xa_in, xb_in, left_ref, right_ref, xa_ref, xb_ref):
+def widen_kernel(xb_in, xa_in, right_ref, left_ref, xb_ref, xa_ref):
     odd = lax.axis_index("gx") % 2 == 1
     for source, ref, high in ((xa_in, xa_ref, jnp.logical_not(odd)), (xb_in, xb_ref, odd)):
         ref[...] = source[...]
@@ -225,10 +225,10 @@
     anow_ref,
     pert_in,
     base_ref,
+    right_ref,
     left_ref,
-    right_ref,
+    xb_ref,
     xa_ref,
-    xb_ref,
     lame_ref,
     shear_ref,
     buoy_ref,
@@ -461,8 +461,8 @@
         name="begin",
     )(*begin_inputs)
 
+    right = lax.ppermute(low, "gy", [(i + 1, i) for i in range(count_y - 1)])
     left = lax.ppermute(high, "gy", [(i, i + 1) for i in range(count_y - 1)])
-    right = lax.ppermute(low, "gy", [(i + 1, i) for i in range(count_y - 1)])
 
     base, xa, xb = pl.pallas_call(
         base_kernel,
@@ -473,14 +473,14 @@
         name="base",
     )(*begin_inputs)
 
-    xa, xb = pl.pallas_call(
+    xb, xa = pl.pallas_call(
         widen_kernel,
         out_shape=(shape(X_ROWS, Z), shape(X_ROWS, Z)),
         in_specs=[VMEM] * 4,
         out_specs=[VMEM] * 2,
         compiler_params=pltpu.CompilerParams(vmem_limit_bytes=4 * 2**20),
         name="widen",
-    )(xa, xb, left, right)
+    )(xb, xa, right, left)
 
     def swap(first):
         pairs = []
@@ -488,8 +488,8 @@
             pairs += [(i, i + 1), (i + 1, i)]
         return pairs
 
+    xb = lax.ppermute(xb, "gx", swap(1))
     xa = lax.ppermute(xa, "gx", swap(0))
-    xb = lax.ppermute(xb, "gx", swap(1))
 
     hess, forward_next, born_next, adjoint_prev = pl.pallas_call(
         functools.partial(step_kernel, count_x, count_y),
@@ -510,10 +510,10 @@
         flat[4],
         pert,
         base,
+        right,
         left,
-        right,
+        xb,
         xa,
-        xb,
         lame,
         shear,
         buoy,

time: 66 us -> 62.3 us (0.944)
  the two profiles are of different devices: /device:TPU:200 before, /device:TPU:512 now
where the time goes in v4:
time: 62.3 us; the launch traced here: 62 us
  blocking collectives  33.3 us (53%)
  starting transfers between devices  11.3 us (18%)
  Pallas kernels  7.73 us (12%)
  waiting for transfers between devices  7.36 us (12%)
  between operations  1.58 us (3%)
  local copies, waits for them, and re-layouts  0.73 us (1%)
    all_to_all x1, blocking collectives, on_device(): lax.all_to_all(hess.reshape(events, CELLS // events, Z), 'event', 0, 0, t...  19.9 us
    all_to_all x1, blocking collectives, on_device(): hess = lax.all_to_all(spread, 'event', 0, 0, tiled=True)  13.4 us
    ppermute x1, starting transfers between devices, on_device(): xa = lax.ppermute(xa, 'gx', swap(0))  4.83 us
    ppermute x1, waiting for transfers between devices, on_device(): left = lax.ppermute(high, 'gy', [(i, i + 1) for i in range(count_y - 1)])  4.62 us
    pallas_call x1, Pallas kernels, on_device(): pl.pallas_call(functools.partial(step_kernel, count_x, count_y), out_shap...  4.11 us
    ppermute x1, starting transfers between devices, on_device(): right = lax.ppermute(low, 'gy', [(i + 1, i) for i in range(count_y - 1)])  3.67 us
    pallas_call x1, Pallas kernels, on_device(): pl.pallas_call(begin_kernel, out_shape=(shape(Y_PLANES, X, Z), shape(Y_PL...  2.75 us
    ppermute x1, waiting for transfers between devices, on_device(): right = lax.ppermute(low, 'gy', [(i + 1, i) for i in range(count_y - 1)])  2.29 us
  transfers between devices with their start and end apart: 4, of which 3 were waited for; matrix products, arithmetic and copies ran while one was open for 0% of the time, Pallas kernels for 1%

profile of v4, /device:TPU:512, one launch (start us, length us, event | category | flops | bytes accessed | tf_op | source)
XLA Modules:
  0.0 62.0 jit_solution(6986427310588791172)
XLA Ops:
  0.6 0.0 copy-start
  0.6 0.0 copy-start.1
  0.7 0.0 copy-start.2
  0.7 0.0 copy-start.3
  0.7 0.0 copy-start.4
  0.7 0.0 copy-start.5
  0.7 0.0 copy-start.6
  0.7 0.0 copy-start.7
  0.7 0.0 copy-start.8
  0.7 0.0 copy-start.9
  0.7 0.0 copy-start.10
  0.7 0.0 copy-start.11
  0.8 0.0 copy-start.12
  0.8 2.8 %begin.1 = (f32[26,16,128]{2,1,0:T(8,128)}, f32[26,16,128]{2,1,0:T(8,128)}) custom-call(f32[3,256,128]{2,1,0:T(8,128)} %bitcast.28, f32[3,256,128]{2,1,0:T(8,128)} %bitcast.19, f32[3,256,128]{2,1,0:T(8,128)} %bitcast.30, f32[3,256,128]{2,1,0:T(8,128)} %bitcast.22, f32[3,256,128]{2,1,0:T(8,128)} %bitcast.25, f32[3,256,128]{2,1,0:T(8,128)} %bitcast.32, ...), custom_call_target="tpu_custom_call" | custom-call | tf_op jit(solution)/shard_map/begin/pallas_call | solution.py:453
  3.5 3.7 %collective-permute-start = (f32[26,16,128]{2,1,0:T(8,128)}, f32[26,16,128]{2,1,0:T(8,128)S(1)}, u32[]{:S(2)}, u32[]{:S(2)}) collective-permute-start(f32[26,16,128]{2,1,0:T(8,128)} %get-tuple-element.16), channel_id=1, source_target_pairs={{1,0},{2,1},{3,2},{4,3},{5,4},{6,5},{7,6},{8,7},{9,8},{10,9},{11,1... | collective-permute-start | bytes 638984 | tf_op jit(solution)/shard_map/ppermute | solution.py:464
  7.2 0.0 copy-start.13
  7.2 2.2 %collective-permute-start.1 = (f32[26,16,128]{2,1,0:T(8,128)}, f32[26,16,128]{2,1,0:T(8,128)S(1)}, u32[]{:S(2)}, u32[]{:S(2)}) collective-permute-start(f32[26,16,128]{2,1,0:T(8,128)} %get-tuple-element.17), channel_id=1, source_target_pairs={{0,1},{1,2},{2,3},{3,4},{4,5},{5,6},{6,7},{7,8},{8,9},{9,10},{10,1... | collective-permute-start | bytes 638984 | tf_op jit(solution)/shard_map/ppermute | solution.py:465
  9.4 0.0 copy-done
  9.4 0.0 copy-done.1
  9.4 0.0 copy-done.2
  9.4 0.0 copy-done.3
  9.4 0.0 copy-done.4
  9.4 0.0 copy-done.5
  9.5 0.0 copy-done.6
  9.5 0.0 copy-done.7
  9.5 0.0 copy-done.8
  9.5 0.0 copy-done.9
  9.5 0.0 copy-done.10
  9.5 0.0 copy-done.11
  9.5 0.0 copy-done.12
  9.5 0.8 %base.1 = (f32[9,256,128]{2,1,0:T(8,128)S(1)}, f32[472,128]{1,0:T(8,128)S(1)}, f32[472,128]{1,0:T(8,128)S(1)}) custom-call(f32[3,256,128]{2,1,0:T(8,128)S(1)} %bitcast.29, f32[3,256,128]{2,1,0:T(8,128)S(1)} %bitcast.20, f32[3,256,128]{2,1,0:T(8,128)S(1)} %bitcast.31, f32[3,256,128]{2,1,0:T(8,128)S(1)} %bitcast.23, f32[3,256,128]{2,1,0:T(8,128)S(1)} %bitcast.26, ...), custom_call_target="tpu_custom_call" | custom-call | tf_op jit(solution)/shard_map/base/pallas_call | solution.py:467
  10.3 2.3 %collective-permute-done.right_ref = f32[26,16,128]{2,1,0:T(8,128)S(1)} collective-permute-done((f32[26,16,128]{2,1,0:T(8,128)}, f32[26,16,128]{2,1,0:T(8,128)S(1)}, u32[]{:S(2)}, u32[]{:S(2)}) %collective-permute-start) | collective-permute-done | bytes 213024 | tf_op jit(solution)/shard_map/ppermute | solution.py:464
  12.6 4.6 %collective-permute-done.1.left_ref = f32[26,16,128]{2,1,0:T(8,128)S(1)} collective-permute-done((f32[26,16,128]{2,1,0:T(8,128)}, f32[26,16,128]{2,1,0:T(8,128)S(1)}, u32[]{:S(2)}, u32[]{:S(2)}) %collective-permute-start.1) | collective-permute-done | bytes 213024 | tf_op jit(solution)/shard_map/ppermute | solution.py:465
  17.2 0.1 widen.1
  17.3 0.7 %collective-permute-start.2 = (f32[472,128]{1,0:T(8,128)S(1)}, f32[472,128]{1,0:T(8,128)S(1)}, u32[]{:S(2)}, u32[]{:S(2)}) collective-permute-start(f32[472,128]{1,0:T(8,128)S(1)} %get-tuple-element.20), channel_id=1, source_target_pairs={{12,24},{24,12},{13,25},{25,13},{14,26},{26,14},{15,27},{27,15},{1... | collective-permute-start | bytes 725000 | tf_op jit(solution)/shard_map/ppermute | solution.py:491
  18.0 4.8 %collective-permute-start.3 = (f32[472,128]{1,0:T(8,128)S(1)}, f32[472,128]{1,0:T(8,128)S(1)}, u32[]{:S(2)}, u32[]{:S(2)}) collective-permute-start(f32[472,128]{1,0:T(8,128)S(1)} %get-tuple-element.21), channel_id=1, source_target_pairs={{0,12},{12,0},{24,36},{36,24},{1,13},{13,1},{25,37},{37,25},{2,14}... | collective-permute-start | bytes 725000 | tf_op jit(solution)/shard_map/ppermute | solution.py:492
  23.5 0.0 collective-permute-done.2.xb_ref
  23.5 0.4 collective-permute-done.3.xa_ref
  24.0 0.0 copy-done.13
  24.0 4.1 %step.1 = (f32[256,128]{1,0:T(8,128)S(1)}, f32[3,256,128]{2,1,0:T(8,128)}, f32[3,256,128]{2,1,0:T(8,128)}, f32[3,256,128]{2,1,0:T(8,128)}) custom-call(f32[3,256,128]{2,1,0:T(8,128)S(1)} %bitcast.21, f32[3,256,128]{2,1,0:T(8,128)S(1)} %bitcast.24, f32[3,256,128]{2,1,0:T(8,128)S(1)} %bitcast.27, f32[256,128]{1,0:T(8,128)S(1)} %bitcast.36, ...), custom_call_target="tpu_custom_call" | custom-call | tf_op jit(solution)/shard_map/step/pallas_call | solution.py:494
  28.1 19.9 %all_to_all.10 = f32[16,16,128]{2,1,0:T(8,128)S(1)} all-to-all(f32[16,16,128]{2,1,0:T(8,128)S(1)} %bitcast.39), channel_id=1, replica_groups=mesh['event'=16,'gx'=4,'gy'=12] {'event'}, dimensions={0} | all-to-all | bytes 262144 | tf_op jit(solution)/shard_map/all_to_all | solution.py:524
  48.0 13.4 %all_to_all.11 = f32[16,16,128]{2,1,0:T(8,128)S(1)} all-to-all(f32[16,16,128]{2,1,0:T(8,128)S(1)} %broadcast_in_dim.2), channel_id=1, replica_groups=mesh['event'=16,'gx'=4,'gy'=12] {'event'}, dimensions={0} | all-to-all | bytes 262144 | tf_op jit(solution)/shard_map/all_to_all | solution.py:527
  61.4 0.7 %copy.21 = f32[16,16,128]{2,1,0:T(8,128)} copy(f32[16,16,128]{2,1,0:T(8,128)S(1)} %all_to_all.11) | data formatting | bytes 262144
  (3 shorter events, 0.0 us)
Async XLA Ops:
  0.6 8.8 %copy-start = (f32[1,3,16,16,128]{4,3,2,1,0:T(8,128)S(1)}, f32[1,3,16,16,128]{4,3,2,1,0:T(8,128)}, u32[]{:S(2)}) copy-start(f32[1,3,16,16,128]{4,3,2,1,0:T(8,128)} %param.16) | copy-start | bytes 1179652
  0.6 8.8 %copy-start.1 = (f32[1,3,16,16,128]{4,3,2,1,0:T(8,128)S(1)}, f32[1,3,16,16,128]{4,3,2,1,0:T(8,128)}, u32[]{:S(2)}) copy-start(f32[1,3,16,16,128]{4,3,2,1,0:T(8,128)} %param.18) | copy-start | bytes 1179652
  0.7 8.8 %copy-start.2 = (f32[1,3,16,16,128]{4,3,2,1,0:T(8,128)S(1)}, f32[1,3,16,16,128]{4,3,2,1,0:T(8,128)}, u32[]{:S(2)}) copy-start(f32[1,3,16,16,128]{4,3,2,1,0:T(8,128)} %param.19) | copy-start | bytes 1179652
  0.7 8.8 %copy-start.3 = (f32[1,3,16,16,128]{4,3,2,1,0:T(8,128)S(1)}, f32[1,3,16,16,128]{4,3,2,1,0:T(8,128)}, u32[]{:S(2)}) copy-start(f32[1,3,16,16,128]{4,3,2,1,0:T(8,128)} %param.15) | copy-start | bytes 1179652
  0.7 8.8 %copy-start.4 = (f32[1,3,16,16,128]{4,3,2,1,0:T(8,128)S(1)}, f32[1,3,16,16,128]{4,3,2,1,0:T(8,128)}, u32[]{:S(2)}) copy-start(f32[1,3,16,16,128]{4,3,2,1,0:T(8,128)} %param.17) | copy-start | bytes 1179652
  0.7 8.8 %copy-start.5 = (f32[1,3,16,16,128]{4,3,2,1,0:T(8,128)S(1)}, f32[1,3,16,16,128]{4,3,2,1,0:T(8,128)}, u32[]{:S(2)}) copy-start(f32[1,3,16,16,128]{4,3,2,1,0:T(8,128)} %param.20) | copy-start | bytes 1179652
  0.7 8.8 %copy-start.6 = (f32[16,16,128]{2,1,0:T(8,128)S(1)}, f32[16,16,128]{2,1,0:T(8,128)}, u32[]{:S(2)}) copy-start(f32[16,16,128]{2,1,0:T(8,128)} %param.21) | copy-start | bytes 393220
  0.7 8.8 %copy-start.7 = (f32[3,3,1,1,1024]{4,3,2,1,0:T(1,128)S(1)}, f32[3,3,1,1,1024]{4,3,2,1,0:T(1,128)}, u32[]{:S(2)}) copy-start(f32[3,3,1,1,1024]{4,3,2,1,0:T(1,128)} %param.26) | copy-start | bytes 110596
  0.7 8.8 %copy-start.8 = (f32[1,3,1,1,1024]{4,3,2,1,0:T(1,128)S(1)}, f32[1,3,1,1,1024]{4,3,2,1,0:T(1,128)}, u32[]{:S(2)}) copy-start(f32[1,3,1,1,1024]{4,3,2,1,0:T(1,128)} %param.27) | copy-start | bytes 36868
  0.7 8.8 %copy-start.9 = (s32[1,1,1024]{2,1,0:T(1,128)S(1)}, s32[1,1,1024]{2,1,0:T(1,128)}, u32[]{:S(2)}) copy-start(s32[1,1,1024]{2,1,0:T(1,128)} %param.25) | copy-start | bytes 12292
  0.7 8.8 %copy-start.10 = (f32[128]{0:T(128)S(1)}, f32[128]{0:T(128)}, u32[]{:S(2)}) copy-start(f32[128]{0:T(128)} %param.24) | copy-start | bytes 1540
  0.7 8.8 %copy-start.11 = (f32[128]{0:T(128)S(1)}, f32[128]{0:T(128)}, u32[]{:S(2)}) copy-start(f32[128]{0:T(128)} %param.22) | copy-start | bytes 1540
  0.8 8.8 %copy-start.12 = (f32[128]{0:T(128)S(1)}, f32[128]{0:T(128)}, u32[]{:S(2)}) copy-start(f32[128]{0:T(128)} %param.23) | copy-start | bytes 1540
  3.5 9.1 %collective-permute-start = (f32[26,16,128]{2,1,0:T(8,128)}, f32[26,16,128]{2,1,0:T(8,128)S(1)}, u32[]{:S(2)}, u32[]{:S(2)}) collective-permute-start(f32[26,16,128]{2,1,0:T(8,128)} %get-tuple-element.16), channel_id=1, source_target_pairs={{1,0},{2,1},{3,2},{4,3},{5,4},{6,5},{7,6},{8,7},{9,8},{10,9},{11,1... | collective-permute-start | bytes 638984 | tf_op jit(solution)/shard_map/ppermute | solution.py:464
  7.2 16.8 %copy-start.13 = (f32[1,3]{1,0:T(1,128)S(1)}, f32[1,3]{1,0:T(1,128)}, u32[]{:S(2)}) copy-start(f32[1,3]{1,0:T(1,128)} %force_ref.1) | copy-start | bytes 40
  7.2 10.0 %collective-permute-start.1 = (f32[26,16,128]{2,1,0:T(8,128)}, f32[26,16,128]{2,1,0:T(8,128)S(1)}, u32[]{:S(2)}, u32[]{:S(2)}) collective-permute-start(f32[26,16,128]{2,1,0:T(8,128)} %get-tuple-element.17), channel_id=1, source_target_pairs={{0,1},{1,2},{2,3},{3,4},{4,5},{5,6},{6,7},{7,8},{8,9},{9,10},{10,1... | collective-permute-start | bytes 638984 | tf_op jit(solution)/shard_map/ppermute | solution.py:465
  17.3 6.2 %collective-permute-start.2 = (f32[472,128]{1,0:T(8,128)S(1)}, f32[472,128]{1,0:T(8,128)S(1)}, u32[]{:S(2)}, u32[]{:S(2)}) collective-permute-start(f32[472,128]{1,0:T(8,128)S(1)} %get-tuple-element.20), channel_id=1, source_target_pairs={{12,24},{24,12},{13,25},{25,13},{14,26},{26,14},{15,27},{27,15},{1... | collective-permute-start | bytes 725000 | tf_op jit(solution)/shard_map/ppermute | solution.py:491
  18.0 6.0 %collective-permute-start.3 = (f32[472,128]{1,0:T(8,128)S(1)}, f32[472,128]{1,0:T(8,128)S(1)}, u32[]{:S(2)}, u32[]{:S(2)}) collective-permute-start(f32[472,128]{1,0:T(8,128)S(1)} %get-tuple-element.21), channel_id=1, source_target_pairs={{0,12},{12,0},{24,36},{36,24},{1,13},{13,1},{25,37},{37,25},{2,14}... | collective-permute-start | bytes 725000 | tf_op jit(solution)/shard_map/ppermute | solution.py:492

commit v5 on v4

--- a/solution.py
+++ b/solution.py
@@ -162,10 +162,13 @@
     motion_ref,
     lame_ref,
     shear_ref,
+    cell_in,
     base_ref,
     xa_ref,
     xb_ref,
+    cell_ref,
 ):
+    cell_ref[...] = cell_in[...]
     columns = lax.broadcasted_iota(jnp.int32, (CELLS, ELEMS), 0)
     applied = placed_force(columns, cells_ref, matrix_ref, motion_ref)
     scale = 0.1 * buoy_ref[...].reshape(1, Z)
@@ -217,7 +220,158 @@
         ref[pl.ds(pert_row(1) + 17, 1), :] = right_ref[Y_PERT, pl.ds(x, 1), :]
 
 
-def step_kernel(
+INNER = (((1, X - 1),), ((2, X - 2),), ((3, X - 3),))
+OUTER = (
+    ((-2, 3), (X - 3, X + 2)),
+    ((-1, 2), (X - 2, X + 1)),
+    ((0, 3), (X - 3, X)),
+)
+
+
+def over(ranges):
+    def run(body):
+        for low, high in ranges:
+            pl.loop(low, high, unroll=high - low)(body)
+
+    return run
+
+
+def sweep(
+    count_x,
+    count_y,
+    stages,
+    base_ref,
+    constants,
+    state,
+    between,
+):
+    first, second, third = stages
+    lame_ref, shear_ref, buoy_ref, cell_ref, force_ref = constants
+    wide, pert, new, born, hess_ref, stress = state
+    index_x, index_y = lax.axis_index("gx"), lax.axis_index("gy")
+    last_x, last_y = count_x - 1, count_y - 1
+
+    def row_mask(first, rows):
+        y = lax.broadcasted_iota(jnp.int32, (rows, Z), 0) + first
+        return ((y >= 0) | (index_y > 0)) & ((y < Y) | (index_y < last_y))
+
+    def plane_valid(x):
+        return ((x >= 0) | (index_x > 0)) & ((x < X) | (index_x < last_x))
+
+    def along_z(value):
+        lane = lax.broadcasted_iota(jnp.int32, value.shape, 1)
+        after = jnp.where(lane < Z - 1, pltpu.roll(value, Z - 1, 1), 0.0)
+        before = jnp.where(lane > 0, pltpu.roll(value, 1, 1), 0.0)
+        return after - before
+
+    def differences(ref, c, row, rows):
+        return (
+            ref[c, pl.ds(row + ROWS, rows), :] - ref[c, pl.ds(row - ROWS, rows), :],
+            ref[c, pl.ds(row + 1, rows), :] - ref[c, pl.ds(row - 1, rows), :],
+            along_z(ref[c, pl.ds(row, rows), :]),
+        )
+
+    wide_mask = row_mask(-2, 24)
+    lame_rows = jnp.where(wide_mask, 0.5 * lame_ref[...].reshape(1, Z), 0.0)
+    shear_rows = jnp.where(wide_mask, shear_ref[...].reshape(1, Z), 0.0)
+
+    @over(first)
+    def _(x):
+        row = (x + 3) * ROWS + ZERO - 2
+        out = (x + 2) * ROWS + ZERO - 2
+        valid = plane_valid(x)
+        lame = jnp.where(valid, lame_rows, 0.0)
+        shear = jnp.where(valid, shear_rows, 0.0)
+        half_shear = 0.5 * shear
+        moved = pert[pl.ds(out, 24), :]
+        half_moved = 0.5 * moved
+        background = None
+        for field in range(3):
+            gx, gy, gz = zip(*[differences(wide, 3 * field + i, row, 24) for i in range(3)])
+            normal = (gx[0], gy[1], gz[2])
+            skew = (gy[0] + gx[1], gz[0] + gx[2], gz[1] + gy[2])
+            if field == 0:
+                background = (normal, skew)
+            volume = lame * (gx[0] + gy[1] + gz[2])
+            for i in range(3):
+                total = shear * normal[i] + volume
+                if field == 1:
+                    total = total + moved * background[0][i]
+                stress[6 * field + i, pl.ds(out, 24), :] = total
+                total = half_shear * skew[i]
+                if field == 1:
+                    total = total + half_moved * background[1][i]
+                stress[6 * field + 3 + i, pl.ds(out, 24), :] = total
+
+    new_mask = row_mask(-1, 24)
+    scale_rows = jnp.where(new_mask, 0.05 * buoy_ref[...].reshape(1, Z), 0.0)
+    top = lax.broadcasted_iota(jnp.int32, (24, Z), 1) == 0
+    point_rows = jnp.where(new_mask, 0.1 * buoy_ref[...].reshape(1, Z), 0.0)
+    received_rows = jnp.where(top, point_rows, 0.0)
+    point = [point_rows * force_ref[:, i : i + 1] for i in range(3)]
+    first_cell = (index_y * Y - 1 + lax.broadcasted_iota(jnp.int32, (24, Z), 0)) * Z
+    source_row = cell_ref[...] - first_cell
+
+    @over(second)
+    def _(x):
+        row = (x + 2) * ROWS + ZERO - 1
+        out = (x + 1) * ROWS + ZERO - 1
+        scale = jnp.where(plane_valid(x), scale_rows, 0.0)
+
+        def across_x(c):
+            return stress[c, pl.ds(row + ROWS, 24), :] - stress[c, pl.ds(row - ROWS, 24), :]
+
+        def across_y(c):
+            return stress[c, pl.ds(row + 1, 24), :] - stress[c, pl.ds(row - 1, 24), :]
+
+        def across_z(c):
+            return along_z(stress[c, pl.ds(row, 24), :])
+
+        change = []
+        for field in range(3):
+            o = 6 * field
+            change.append(
+                (
+                    scale * (across_x(o) + across_y(o + 3) + across_z(o + 4)),
+                    scale * (across_x(o + 3) + across_y(o + 1) + across_z(o + 5)),
+                    scale * (across_x(o + 4) + across_y(o + 5) + across_z(o + 2)),
+                )
+            )
+        here = source_row == (index_x * X + x) * (count_y * Y * Z)
+        for i in range(3):
+            new[i, pl.ds(out, 24), :] = new[i, pl.ds(out, 24), :] + (
+                change[0][i] + jnp.where(here, point[i], 0.0)
+            )
+            new[3 + i, pl.ds(out, 24), :] = new[3 + i, pl.ds(out, 24), :] + (
+                change[2][i] + received_rows * change[1][i]
+            )
+
+        @pl.when((x >= 0) & (x < X))
+        def _():
+            at = pl.multiple_of(x * Y, Y)
+            for i in range(3):
+                born[i, pl.ds(at, Y), :] = (
+                    base_ref[3 + i, pl.ds(at, Y), :] + change[1][i][1 : Y + 1]
+                )
+
+    between()
+
+    @over(third)
+    def _(x):
+        row = pl.multiple_of((x + 1) * ROWS + ZERO, 8)
+        at = pl.multiple_of(x * Y, Y)
+        hx, hy, hz = zip(*[differences(new, i, row, Y) for i in range(3)])
+        kx, ky, kz = zip(*[differences(new, 3 + i, row, Y) for i in range(3)])
+        normal = hx[0] * kx[0] + hy[1] * ky[1] + hz[2] * kz[2]
+        skew = (
+            (hy[0] + hx[1]) * (ky[0] + kx[1])
+            + (hz[0] + hx[2]) * (kz[0] + kx[2])
+            + (hz[1] + hy[2]) * (kz[1] + ky[2])
+        )
+        hess_ref[pl.ds(at, Y), :] = -0.0125 * (2.0 * normal + skew)
+
+
+def inner_kernel(
     count_x,
     count_y,
     fnow_ref,
@@ -227,25 +381,10 @@
     base_ref,
     right_ref,
     left_ref,
-    xb_ref,
-    xa_ref,
-    lame_ref,
-    shear_ref,
-    buoy_ref,
-    cell_ref,
-    force_ref,
-    hess_ref,
-    fnext_ref,
-    bnext_ref,
-    aprev_ref,
-    wide,
-    pert,
-    stress,
-    new,
+    *refs,
 ):
-    index_x, index_y = lax.axis_index("gx"), lax.axis_index("gy")
-    last_x, last_y = count_x - 1, count_y - 1
-
+    constants, state = refs[:5], refs[5:]
+    wide, pert, new, born, hess_ref, stress = state
     now = [r.at[i] for r in (fnow_ref, bnow_ref, anow_ref) for i in range(3)]
     for c in range(9):
         for x in range(X):
@@ -267,6 +406,15 @@
             new[c, pl.ds((x + 1) * ROWS + ZERO, Y), :] = base_ref[b, pl.ds(x * Y, Y), :]
         new[c, pl.ds(ROWS + ZERO - 1, X, stride=ROWS), :] = left_ref[Y_BASE + c]
         new[c, pl.ds(ROWS + ZERO + Y, X, stride=ROWS), :] = right_ref[Y_BASE + c]
+    sweep(count_x, count_y, INNER, base_ref, constants, state, lambda: None)
+
+
+def step_kernel(count_x, count_y, base_ref, xb_ref, xa_ref, *refs):
+    constants, refs = refs[:5], refs[10:]
+    wide, pert, new, born, hess_ref = refs[:5]
+    fnext_ref, bnext_ref, aprev_ref, stress, sent = refs[5:]
+    state = (*refs[:5], stress)
+    index_x = lax.axis_index("gx")
     odd = index_x % 2 == 1
     for ref, high in ((xa_ref, jnp.logical_not(odd)), (xb_ref, odd)):
         for d in (1, 2):
@@ -283,125 +431,22 @@
                 for c in range(6):
                     new[c, pl.ds((x + 1) * ROWS + ZERO, Y), :] = ref[pl.ds(X_BASE + c * Y, Y), :]
 
-    def row_mask(first, rows):
-        y = lax.broadcasted_iota(jnp.int32, (rows, Z), 0) + first
-        return ((y >= 0) | (index_y > 0)) & ((y < Y) | (index_y < last_y))
-
-    def plane_valid(x):
-        return ((x >= 0) | (index_x > 0)) & ((x < X) | (index_x < last_x))
-
-    def along_z(value):
-        lane = lax.broadcasted_iota(jnp.int32, value.shape, 1)
-        after = jnp.where(lane < Z - 1, pltpu.roll(value, Z - 1, 1), 0.0)
-        before = jnp.where(lane > 0, pltpu.roll(value, 1, 1), 0.0)
-        return after - before
-
-    def differences(ref, c, row, rows):
-        return (
-            ref[c, pl.ds(row + ROWS, rows), :] - ref[c, pl.ds(row - ROWS, rows), :],
-            ref[c, pl.ds(row + 1, rows), :] - ref[c, pl.ds(row - 1, rows), :],
-            along_z(ref[c, pl.ds(row, rows), :]),
+    inner = new.reshape(6, X + 2, ROWS, Z)
+    copies = [
+        pltpu.make_async_copy(
+            inner.at[pl.ds(first, 3), pl.ds(1, X), pl.ds(ZERO, Y), :], ref, sent.at[k]
         )
-
-    wide_mask = row_mask(-2, 24)
-    lame_rows = jnp.where(wide_mask, 0.5 * lame_ref[...].reshape(1, Z), 0.0)
-    shear_rows = jnp.where(wide_mask, shear_ref[...].reshape(1, Z), 0.0)
-
-    @pl.loop(-2, X + 2, unroll=X + 4)
-    def _(x):
-        row = (x + 3) * ROWS + ZERO - 2
-        out = (x + 2) * ROWS + ZERO - 2
-        valid = plane_valid(x)
-        lame = jnp.where(valid, lame_rows, 0.0)
-        shear = jnp.where(valid, shear_rows, 0.0)
-        half_shear = 0.5 * shear
-        moved = pert[pl.ds(out, 24), :]
-        half_moved = 0.5 * moved
-        first = None
-        for field in range(3):
-            gx, gy, gz = zip(*[differences(wide, 3 * field + i, row, 24) for i in range(3)])
-            normal = (gx[0], gy[1], gz[2])
-            skew = (gy[0] + gx[1], gz[0] + gx[2], gz[1] + gy[2])
-            if field == 0:
-                first = (normal, skew)
-            volume = lame * (gx[0] + gy[1] + gz[2])
-            for i in range(3):
-                total = shear * normal[i] + volume
-                if field == 1:
-                    total = total + moved * first[0][i]
-                stress[6 * field + i, pl.ds(out, 24), :] = total
-                total = half_shear * skew[i]
-                if field == 1:
-                    total = total + half_moved * first[1][i]
-                stress[6 * field + 3 + i, pl.ds(out, 24), :] = total
-
-    new_mask = row_mask(-1, 24)
-    scale_rows = jnp.where(new_mask, 0.05 * buoy_ref[...].reshape(1, Z), 0.0)
-    top = lax.broadcasted_iota(jnp.int32, (24, Z), 1) == 0
-    point_rows = jnp.where(new_mask, 0.1 * buoy_ref[...].reshape(1, Z), 0.0)
-    received_rows = jnp.where(top, point_rows, 0.0)
-    point = [point_rows * force_ref[:, i : i + 1] for i in range(3)]
-    first_cell = (index_y * Y - 1 + lax.broadcasted_iota(jnp.int32, (24, Z), 0)) * Z
-    source_row = cell_ref[...] - first_cell
-
-    @pl.loop(-1, X + 1, unroll=X + 2)
-    def _(x):
-        row = (x + 2) * ROWS + ZERO - 1
-        out = (x + 1) * ROWS + ZERO - 1
-        scale = jnp.where(plane_valid(x), scale_rows, 0.0)
-
-        def across_x(c):
-            return stress[c, pl.ds(row + ROWS, 24), :] - stress[c, pl.ds(row - ROWS, 24), :]
-
-        def across_y(c):
-            return stress[c, pl.ds(row + 1, 24), :] - stress[c, pl.ds(row - 1, 24), :]
-
-        def across_z(c):
-            return along_z(stress[c, pl.ds(row, 24), :])
-
-        change = []
-        for field in range(3):
-            o = 6 * field
-            change.append(
-                (
-                    scale * (across_x(o) + across_y(o + 3) + across_z(o + 4)),
-                    scale * (across_x(o + 3) + across_y(o + 1) + across_z(o + 5)),
-                    scale * (across_x(o + 4) + across_y(o + 5) + across_z(o + 2)),
-                )
-            )
-        here = source_row == (index_x * X + x) * (count_y * Y * Z)
-        for i in range(3):
-            new[i, pl.ds(out, 24), :] = new[i, pl.ds(out, 24), :] + (
-                change[0][i] + jnp.where(here, point[i], 0.0)
-            )
-            new[3 + i, pl.ds(out, 24), :] = new[3 + i, pl.ds(out, 24), :] + (
-                change[2][i] + received_rows * change[1][i]
-            )
-
-        @pl.when((x >= 0) & (x < X))
-        def _():
-            at = pl.multiple_of(x * Y, Y)
-            for i in range(3):
-                bnext_ref[i, pl.ds(at, Y), :] = (
-                    base_ref[3 + i, pl.ds(at, Y), :] + change[1][i][1 : Y + 1]
-                )
-
-    @pl.loop(0, X, unroll=X)
-    def _(x):
-        row = pl.multiple_of((x + 1) * ROWS + ZERO, 8)
-        at = pl.multiple_of(x * Y, Y)
-        for i in range(3):
-            fnext_ref[i, pl.ds(at, Y), :] = new[i, pl.ds(row, Y), :]
-            aprev_ref[i, pl.ds(at, Y), :] = new[3 + i, pl.ds(row, Y), :]
-        hx, hy, hz = zip(*[differences(new, i, row, Y) for i in range(3)])
-        kx, ky, kz = zip(*[differences(new, 3 + i, row, Y) for i in range(3)])
-        normal = hx[0] * kx[0] + hy[1] * ky[1] + hz[2] * kz[2]
-        skew = (
-            (hy[0] + hx[1]) * (ky[0] + kx[1])
-            + (hz[0] + hx[2]) * (kz[0] + kx[2])
-            + (hz[1] + hy[2]) * (kz[1] + ky[2])
-        )
-        hess_ref[pl.ds(at, Y), :] = -0.0125 * (2.0 * normal + skew)
+        for k, (first, ref) in enumerate(((0, fnext_ref), (3, aprev_ref)))
+    ] + [pltpu.make_async_copy(born, bnext_ref, sent.at[2])]
+
+    def send():
+        for copy in copies:
+            copy.start()
+
+    sweep(count_x, count_y, OUTER, base_ref, constants, state, send)
+
+    for copy in copies:
+        copy.wait()
 
 
 def shape(*dims):
@@ -464,14 +509,19 @@
     right = lax.ppermute(low, "gy", [(i + 1, i) for i in range(count_y - 1)])
     left = lax.ppermute(high, "gy", [(i, i + 1) for i in range(count_y - 1)])
 
-    base, xa, xb = pl.pallas_call(
+    base, xa, xb, cell = pl.pallas_call(
         base_kernel,
-        out_shape=(shape(9, CELLS, Z), shape(X_ROWS, Z), shape(X_ROWS, Z)),
-        in_specs=[VMEM] * 13,
-        out_specs=[VMEM] * 3,
+        out_shape=(
+            shape(9, CELLS, Z),
+            shape(X_ROWS, Z),
+            shape(X_ROWS, Z),
+            jax.ShapeDtypeStruct((1, Z), jnp.int32),
+        ),
+        in_specs=[VMEM] * 14,
+        out_specs=[VMEM] * 4,
         compiler_params=pltpu.CompilerParams(vmem_limit_bytes=16 * 2**20),
         name="base",
-    )(*begin_inputs)
+    )(*begin_inputs, source_cell[:, None] - lax.broadcasted_iota(jnp.int32, (1, Z), 1))
 
     xb, xa = pl.pallas_call(
         widen_kernel,
@@ -491,35 +541,37 @@
     xb = lax.ppermute(xb, "gx", swap(1))
     xa = lax.ppermute(xa, "gx", swap(0))
 
-    hess, forward_next, born_next, adjoint_prev = pl.pallas_call(
+    constants = (lame, shear, buoy, cell, source_force)
+    held = (
+        shape(9, (X + 6) * ROWS, Z),
+        shape((X + 4) * ROWS, Z),
+        shape(6, (X + 2) * ROWS, Z),
+        shape(3, CELLS, Z),
+        shape(CELLS, Z),
+    )
+    state = pl.pallas_call(
+        functools.partial(inner_kernel, count_x, count_y),
+        out_shape=held,
+        in_specs=[VMEM] * 12,
+        out_specs=[VMEM] * 5,
+        scratch_shapes=[pltpu.VMEM((18, (X + 4) * ROWS, Z), F32)],
+        compiler_params=pltpu.CompilerParams(vmem_limit_bytes=24 * 2**20),
+        name="inner",
+    )(flat[1], flat[3], flat[4], pert, base, right, left, *constants)
+
+    *_, hess, forward_next, born_next, adjoint_prev = pl.pallas_call(
         functools.partial(step_kernel, count_x, count_y),
-        out_shape=(shape(CELLS, Z), shape(3, CELLS, Z), shape(3, CELLS, Z), shape(3, CELLS, Z)),
-        in_specs=[VMEM] * 14,
-        out_specs=[VMEM] * 4,
+        out_shape=held + (shape(3, X, Y, Z), shape(3, CELLS, Z), shape(3, X, Y, Z)),
+        in_specs=[VMEM] * 13,
+        out_specs=[VMEM] * 5 + [HBM] * 3,
         scratch_shapes=[
-            pltpu.VMEM((9, (X + 6) * ROWS, Z), F32),
-            pltpu.VMEM(((X + 4) * ROWS, Z), F32),
             pltpu.VMEM((18, (X + 4) * ROWS, Z), F32),
-            pltpu.VMEM((6, (X + 2) * ROWS, Z), F32),
+            pltpu.SemaphoreType.DMA((3,)),
         ],
-        compiler_params=pltpu.CompilerParams(vmem_limit_bytes=20 * 2**20),
+        input_output_aliases={8 + i: i for i in range(5)},
+        compiler_params=pltpu.CompilerParams(vmem_limit_bytes=24 * 2**20),
         name="step",
-    )(
-        flat[1],
-        flat[3],
-        flat[4],
-        pert,
-        base,
-        right,
-        left,
-        xb,
-        xa,
-        lame,
-        shear,
-        buoy,
-        source_cell[:, None] - lax.broadcasted_iota(jnp.int32, (1, Z), 1),
-        source_force,
-    )
+    )(base, xb, xa, *constants, *state)
 
     parts = lax.all_to_all(hess.reshape(events, CELLS // events, Z), "event", 0, 0, tiled=True)
     part = jnp.sum(parts, axis=0)

time: 62.3 us -> 60.8 us (0.976)
  waiting for transfers between devices: 7.36 us -> 6.26 us
  blocking collectives: 33.3 us -> 32.4 us
    pallas_call x0 -> x1, Pallas kernels: none -> 2.33 us  [on_device(): pl.pallas_call(functools.partial(inner_kernel, count_x, count_y), out_sha...]
    pallas_call x1, Pallas kernels: 4.11 us -> 2.14 us  [on_device(): pl.pallas_call(functools.partial(step_kernel, count_x, count_y), out_shap...]
    all_to_all x1, blocking collectives: 19.9 us -> 19.1 us  [on_device(): lax.all_to_all(hess.reshape(events, CELLS // events, Z), 'event', 0, 0, t...]
    ppermute x1, waiting for transfers between devices: 2.29 us -> 1.64 us  [on_device(): right = lax.ppermute(low, 'gy', [(i + 1, i) for i in range(count_y - 1)])]
  transfers between devices with their start and end apart: 4 -> 4, of which waited for: 3 -> 2; matrix products, arithmetic and copies ran while one was open for 0% -> 0% of each run, Pallas kernels for 1% -> 5%
where the time goes in v5:
time: 60.8 us; the launch traced here: 60.5 us
  blocking collectives  32.4 us (53%)
  starting transfers between devices  11.4 us (19%)
  Pallas kernels  8.13 us (13%)
  waiting for transfers between devices  6.26 us (10%)
  between operations  1.61 us (3%)
  local copies, waits for them, and re-layouts  0.73 us (1%)
    all_to_all x1, blocking collectives, on_device(): lax.all_to_all(hess.reshape(events, CELLS // events, Z), 'event', 0, 0, t...  19.1 us
    all_to_all x1, blocking collectives, on_device(): hess = lax.all_to_all(spread, 'event', 0, 0, tiled=True)  13.3 us
    ppermute x1, starting transfers between devices, on_device(): xa = lax.ppermute(xa, 'gx', swap(0))  4.83 us
    ppermute x1, waiting for transfers between devices, on_device(): left = lax.ppermute(high, 'gy', [(i, i + 1) for i in range(count_y - 1)])  4.61 us
    ppermute x1, starting transfers between devices, on_device(): right = lax.ppermute(low, 'gy', [(i + 1, i) for i in range(count_y - 1)])  3.67 us
    pallas_call x1, Pallas kernels, on_device(): pl.pallas_call(begin_kernel, out_shape=(shape(Y_PLANES, X, Z), shape(Y_PL...  2.78 us
    pallas_call x1, Pallas kernels, on_device(): pl.pallas_call(functools.partial(inner_kernel, count_x, count_y), out_sha...  2.33 us
    ppermute x1, starting transfers between devices, on_device(): left = lax.ppermute(high, 'gy', [(i, i + 1) for i in range(count_y - 1)])  2.17 us
  transfers between devices with their start and end apart: 4, of which 2 were waited for; matrix products, arithmetic and copies ran while one was open for 0% of the time, Pallas kernels for 5%

profile of v5, /device:TPU:512, one launch (start us, length us, event | category | flops | bytes accessed | tf_op | source)
XLA Modules:
  0.0 60.5 jit_solution(5189484526178035193)
XLA Ops:
  0.6 0.0 copy-start.8
  0.6 0.0 copy-start.7
  0.7 0.0 copy-start.9
  0.7 0.0 copy-start.10
  0.7 0.0 copy-start.12
  0.7 0.0 copy-start.11
  0.7 0.0 copy-start.6
  0.7 0.0 copy-start.5
  0.7 0.0 copy-start.2
  0.7 0.0 copy-start.1
  0.7 0.0 copy-start.4
  0.7 0.0 copy-start
  0.8 0.0 copy-start.3
  0.8 2.8 %begin.1 = (f32[26,16,128]{2,1,0:T(8,128)}, f32[26,16,128]{2,1,0:T(8,128)}) custom-call(f32[3,256,128]{2,1,0:T(8,128)} %bitcast.28, f32[3,256,128]{2,1,0:T(8,128)} %bitcast.19, f32[3,256,128]{2,1,0:T(8,128)} %bitcast.30, f32[3,256,128]{2,1,0:T(8,128)} %bitcast.22, f32[3,256,128]{2,1,0:T(8,128)} %bitcast.25, f32[3,256,128]{2,1,0:T(8,128)} %bitcast.32, ...), custom_call_target="tpu_custom_call" | custom-call | tf_op jit(solution)/shard_map/begin/pallas_call | solution.py:498
  3.6 0.0 copy-start.13
  3.6 3.7 %collective-permute-start = (f32[26,16,128]{2,1,0:T(8,128)}, f32[26,16,128]{2,1,0:T(8,128)S(1)}, u32[]{:S(2)}, u32[]{:S(2)}) collective-permute-start(f32[26,16,128]{2,1,0:T(8,128)} %get-tuple-element.24), channel_id=1, source_target_pairs={{1,0},{2,1},{3,2},{4,3},{5,4},{6,5},{7,6},{8,7},{9,8},{10,9},{11,1... | collective-permute-start | bytes 638984 | tf_op jit(solution)/shard_map/ppermute | solution.py:509
  7.2 2.2 %collective-permute-start.1 = (f32[26,16,128]{2,1,0:T(8,128)}, f32[26,16,128]{2,1,0:T(8,128)S(1)}, u32[]{:S(2)}, u32[]{:S(2)}) collective-permute-start(f32[26,16,128]{2,1,0:T(8,128)} %get-tuple-element.25), channel_id=1, source_target_pairs={{0,1},{1,2},{2,3},{3,4},{4,5},{5,6},{6,7},{7,8},{8,9},{9,10},{10,1... | collective-permute-start | bytes 638984 | tf_op jit(solution)/shard_map/ppermute | solution.py:510
  10.1 0.0 copy-done.8
  10.1 0.0 copy-done.7
  10.1 0.0 copy-done.9
  10.1 0.0 copy-done.10
  10.1 0.0 copy-done.12
  10.1 0.0 copy-done.11
  10.1 0.0 copy-done.6
  10.2 0.0 copy-done.5
  10.2 0.0 copy-done.2
  10.2 0.0 copy-done.1
  10.2 0.0 copy-done.4
  10.2 0.0 copy-done
  10.2 0.0 copy-done.3
  10.2 0.8 %base.1 = (f32[9,256,128]{2,1,0:T(8,128)S(1)}, f32[472,128]{1,0:T(8,128)S(1)}, f32[472,128]{1,0:T(8,128)S(1)}, s32[1,128]{1,0:T(1,128)S(1)}) custom-call(f32[3,256,128]{2,1,0:T(8,128)S(1)} %bitcast.29, f32[3,256,128]{2,1,0:T(8,128)S(1)} %bitcast.20, f32[3,256,128]{2,1,0:T(8,128)S(1)} %bitcast.31, f32[3,256,128]{2,1,0:T(8,128)S(1)} %bitcast.23, ...), custom_call_target="tpu_custom_call" | custom-call | tf_op jit(solution)/shard_map/base/pallas_call | solution.py:512
  11.0 1.6 %collective-permute-done.right_ref = f32[26,16,128]{2,1,0:T(8,128)S(1)} collective-permute-done((f32[26,16,128]{2,1,0:T(8,128)}, f32[26,16,128]{2,1,0:T(8,128)S(1)}, u32[]{:S(2)}, u32[]{:S(2)}) %collective-permute-start) | collective-permute-done | bytes 213024 | tf_op jit(solution)/shard_map/ppermute | solution.py:509
  12.7 4.6 %collective-permute-done.1.left_ref = f32[26,16,128]{2,1,0:T(8,128)S(1)} collective-permute-done((f32[26,16,128]{2,1,0:T(8,128)}, f32[26,16,128]{2,1,0:T(8,128)S(1)}, u32[]{:S(2)}, u32[]{:S(2)}) %collective-permute-start.1) | collective-permute-done | bytes 213024 | tf_op jit(solution)/shard_map/ppermute | solution.py:510
  17.3 0.1 widen.1
  17.3 0.7 %collective-permute-start.2 = (f32[472,128]{1,0:T(8,128)S(1)}, f32[472,128]{1,0:T(8,128)S(1)}, u32[]{:S(2)}, u32[]{:S(2)}) collective-permute-start(f32[472,128]{1,0:T(8,128)S(1)} %get-tuple-element.26), channel_id=1, source_target_pairs={{12,24},{24,12},{13,25},{25,13},{14,26},{26,14},{15,27},{27,15},{1... | collective-permute-start | bytes 725000 | tf_op jit(solution)/shard_map/ppermute | solution.py:541
  18.0 4.8 %collective-permute-start.3 = (f32[472,128]{1,0:T(8,128)S(1)}, f32[472,128]{1,0:T(8,128)S(1)}, u32[]{:S(2)}, u32[]{:S(2)}) collective-permute-start(f32[472,128]{1,0:T(8,128)S(1)} %get-tuple-element.27), channel_id=1, source_target_pairs={{0,12},{12,0},{24,36},{36,24},{1,13},{13,1},{25,37},{37,25},{2,14}... | collective-permute-start | bytes 725000 | tf_op jit(solution)/shard_map/ppermute | solution.py:542
  22.9 0.0 copy-done.13
  22.9 2.3 %inner.1 = (f32[9,704,128]{2,1,0:T(8,128)S(1)}, f32[640,128]{1,0:T(8,128)S(1)}, f32[6,576,128]{2,1,0:T(8,128)S(1)}, f32[3,256,128]{2,1,0:T(8,128)S(1)}, f32[256,128]{1,0:T(8,128)S(1)}) custom-call(f32[3,256,128]{2,1,0:T(8,128)S(1)} %bitcast.21, f32[3,256,128]{2,1,0:T(8,128)S(1)} %bitcast.24, f32[3,256,128]{2,1,0:T(8,128)S(1)} %bitcast.27, ...), custom_call_target="tpu_custom_call" | custom-call | tf_op jit(solution)/shard_map/inner/pallas_call | solution.py:552
  25.2 0.0 collective-permute-done.2.xb_ref
  25.2 0.0 collective-permute-done.3.xa_ref
  25.2 2.1 %step.1 = (f32[9,704,128]{2,1,0:T(8,128)S(1)}, f32[640,128]{1,0:T(8,128)S(1)}, f32[6,576,128]{2,1,0:T(8,128)S(1)}, f32[3,256,128]{2,1,0:T(8,128)S(1)}, f32[256,1...) custom-call(f32[9,256,128]{2,1,0:T(8,128)S(1)} %get-tuple-element.21, ...), custom_call_target="tpu_custom_call", output_to_operand_aliasing={{0}: (8, {}), {1}: (9, {}), {2}: (10, {}), {3}: (11, {}), {... | custom-call | tf_op jit(solution)/shard_map/step/pallas_call | solution.py:562
  27.4 19.1 %all_to_all.10 = f32[16,16,128]{2,1,0:T(8,128)S(1)} all-to-all(f32[16,16,128]{2,1,0:T(8,128)S(1)} %bitcast.37), channel_id=1, replica_groups=mesh['event'=16,'gx'=4,'gy'=12] {'event'}, dimensions={0} | all-to-all | bytes 262144 | tf_op jit(solution)/shard_map/all_to_all | solution.py:576
  46.6 13.3 %all_to_all.11 = f32[16,16,128]{2,1,0:T(8,128)S(1)} all-to-all(f32[16,16,128]{2,1,0:T(8,128)S(1)} %broadcast_in_dim.2), channel_id=1, replica_groups=mesh['event'=16,'gx'=4,'gy'=12] {'event'}, dimensions={0} | all-to-all | bytes 262144 | tf_op jit(solution)/shard_map/all_to_all | solution.py:579
  59.9 0.7 %copy.31 = f32[16,16,128]{2,1,0:T(8,128)} copy(f32[16,16,128]{2,1,0:T(8,128)S(1)} %all_to_all.11) | data formatting | bytes 262144
  (3 shorter events, 0.0 us)
Async XLA Ops:
  0.6 9.4 %copy-start.8 = (f32[1,3,1,1,1024]{4,3,2,1,0:T(1,128)S(1)}, f32[1,3,1,1,1024]{4,3,2,1,0:T(1,128)}, u32[]{:S(2)}) copy-start(f32[1,3,1,1,1024]{4,3,2,1,0:T(1,128)} %param.27) | copy-start | bytes 36868
  0.6 9.4 %copy-start.7 = (f32[3,3,1,1,1024]{4,3,2,1,0:T(1,128)S(1)}, f32[3,3,1,1,1024]{4,3,2,1,0:T(1,128)}, u32[]{:S(2)}) copy-start(f32[3,3,1,1,1024]{4,3,2,1,0:T(1,128)} %param.26) | copy-start | bytes 110596
  0.7 9.4 %copy-start.9 = (s32[1,1,1024]{2,1,0:T(1,128)S(1)}, s32[1,1,1024]{2,1,0:T(1,128)}, u32[]{:S(2)}) copy-start(s32[1,1,1024]{2,1,0:T(1,128)} %param.25) | copy-start | bytes 12292
  0.7 9.4 %copy-start.10 = (f32[128]{0:T(128)S(1)}, f32[128]{0:T(128)}, u32[]{:S(2)}) copy-start(f32[128]{0:T(128)} %param.24) | copy-start | bytes 1540
  0.7 9.4 %copy-start.12 = (f32[128]{0:T(128)S(1)}, f32[128]{0:T(128)}, u32[]{:S(2)}) copy-start(f32[128]{0:T(128)} %param.23) | copy-start | bytes 1540
  0.7 9.4 %copy-start.11 = (f32[128]{0:T(128)S(1)}, f32[128]{0:T(128)}, u32[]{:S(2)}) copy-start(f32[128]{0:T(128)} %param.22) | copy-start | bytes 1540
  0.7 9.4 %copy-start.6 = (f32[16,16,128]{2,1,0:T(8,128)S(1)}, f32[16,16,128]{2,1,0:T(8,128)}, u32[]{:S(2)}) copy-start(f32[16,16,128]{2,1,0:T(8,128)} %param.21) | copy-start | bytes 393220
  0.7 9.4 %copy-start.5 = (f32[1,3,16,16,128]{4,3,2,1,0:T(8,128)S(1)}, f32[1,3,16,16,128]{4,3,2,1,0:T(8,128)}, u32[]{:S(2)}) copy-start(f32[1,3,16,16,128]{4,3,2,1,0:T(8,128)} %param.20) | copy-start | bytes 1179652
  0.7 9.4 %copy-start.2 = (f32[1,3,16,16,128]{4,3,2,1,0:T(8,128)S(1)}, f32[1,3,16,16,128]{4,3,2,1,0:T(8,128)}, u32[]{:S(2)}) copy-start(f32[1,3,16,16,128]{4,3,2,1,0:T(8,128)} %param.19) | copy-start | bytes 1179652
  0.7 9.4 %copy-start.1 = (f32[1,3,16,16,128]{4,3,2,1,0:T(8,128)S(1)}, f32[1,3,16,16,128]{4,3,2,1,0:T(8,128)}, u32[]{:S(2)}) copy-start(f32[1,3,16,16,128]{4,3,2,1,0:T(8,128)} %param.18) | copy-start | bytes 1179652
  0.7 9.4 %copy-start.4 = (f32[1,3,16,16,128]{4,3,2,1,0:T(8,128)S(1)}, f32[1,3,16,16,128]{4,3,2,1,0:T(8,128)}, u32[]{:S(2)}) copy-start(f32[1,3,16,16,128]{4,3,2,1,0:T(8,128)} %param.17) | copy-start | bytes 1179652
  0.7 9.4 %copy-start = (f32[1,3,16,16,128]{4,3,2,1,0:T(8,128)S(1)}, f32[1,3,16,16,128]{4,3,2,1,0:T(8,128)}, u32[]{:S(2)}) copy-start(f32[1,3,16,16,128]{4,3,2,1,0:T(8,128)} %param.16) | copy-start | bytes 1179652
  0.8 9.4 %copy-start.3 = (f32[1,3,16,16,128]{4,3,2,1,0:T(8,128)S(1)}, f32[1,3,16,16,128]{4,3,2,1,0:T(8,128)}, u32[]{:S(2)}) copy-start(f32[1,3,16,16,128]{4,3,2,1,0:T(8,128)} %param.15) | copy-start | bytes 1179652
  3.6 19.3 %copy-start.13 = (f32[1,3]{1,0:T(1,128)S(1)}, f32[1,3]{1,0:T(1,128)}, u32[]{:S(2)}) copy-start(f32[1,3]{1,0:T(1,128)} %refs_4_.3) | copy-start | bytes 40
  3.6 9.1 %collective-permute-start = (f32[26,16,128]{2,1,0:T(8,128)}, f32[26,16,128]{2,1,0:T(8,128)S(1)}, u32[]{:S(2)}, u32[]{:S(2)}) collective-permute-start(f32[26,16,128]{2,1,0:T(8,128)} %get-tuple-element.24), channel_id=1, source_target_pairs={{1,0},{2,1},{3,2},{4,3},{5,4},{6,5},{7,6},{8,7},{9,8},{10,9},{11,1... | collective-permute-start | bytes 638984 | tf_op jit(solution)/shard_map/ppermute | solution.py:509
  7.2 10.0 %collective-permute-start.1 = (f32[26,16,128]{2,1,0:T(8,128)}, f32[26,16,128]{2,1,0:T(8,128)S(1)}, u32[]{:S(2)}, u32[]{:S(2)}) collective-permute-start(f32[26,16,128]{2,1,0:T(8,128)} %get-tuple-element.25), channel_id=1, source_target_pairs={{0,1},{1,2},{2,3},{3,4},{4,5},{5,6},{6,7},{7,8},{8,9},{9,10},{10,1... | collective-permute-start | bytes 638984 | tf_op jit(solution)/shard_map/ppermute | solution.py:510
  17.3 7.9 %collective-permute-start.2 = (f32[472,128]{1,0:T(8,128)S(1)}, f32[472,128]{1,0:T(8,128)S(1)}, u32[]{:S(2)}, u32[]{:S(2)}) collective-permute-start(f32[472,128]{1,0:T(8,128)S(1)} %get-tuple-element.26), channel_id=1, source_target_pairs={{12,24},{24,12},{13,25},{25,13},{14,26},{26,14},{15,27},{27,15},{1... | collective-permute-start | bytes 725000 | tf_op jit(solution)/shard_map/ppermute | solution.py:541
  18.0 7.2 %collective-permute-start.3 = (f32[472,128]{1,0:T(8,128)S(1)}, f32[472,128]{1,0:T(8,128)S(1)}, u32[]{:S(2)}, u32[]{:S(2)}) collective-permute-start(f32[472,128]{1,0:T(8,128)S(1)} %get-tuple-element.27), channel_id=1, source_target_pairs={{0,12},{12,0},{24,36},{36,24},{1,13},{13,1},{25,37},{37,25},{2,14}... | collective-permute-start | bytes 725000 | tf_op jit(solution)/shard_map/ppermute | solution.py:542
